TPU v7x, 32 devices: a whole 2x2x4 slice. The times are simulated.
32 devices in a mesh: dp: 4 (over y, x), fsdp: 8 (over z, core).
Axes of the slice: x: 2, y: 2, z: 4, core: 2. Of those that a mesh axis runs over, the one named last changes fastest.
Arguments:
- feats: bfloat16 [192, 196, 1024], P(('dp', 'fsdp')), may hold values from -6 to 6
- text: bfloat16 [192, 64, 768], P(('dp', 'fsdp')), may hold values from -6 to 6
- lengths: int32 [192], P(('dp', 'fsdp')), may hold values from 1 to 64, as said below
- cotangent: bfloat16 [192, 260, 768], P(('dp', 'fsdp')), may hold values from -6 to 6
- w_red: bfloat16 [1024, 256], P(('dp', 'fsdp')), may hold values from -0.1875 to 0.1875
- bn1_gain: bfloat16 [256], P(('dp', 'fsdp')), may hold values from 0.5 to 1.5
- bn1_bias: bfloat16 [256], P(('dp', 'fsdp')), may hold values from -3 to 3
- w_conv: bfloat16 [2304, 256], P(('dp', 'fsdp')), may hold values from -0.125 to 0.125
- bn2_gain: bfloat16 [256], P(('dp', 'fsdp')), may hold values from 0.5 to 1.5
- bn2_bias: bfloat16 [256], P(('dp', 'fsdp')), may hold values from -3 to 3
- w_exp: bfloat16 [256, 1024], P(('dp', 'fsdp')), may hold values from -0.375 to 0.375
- bn3_gain: bfloat16 [1024], P(('dp', 'fsdp')), may hold values from 0.5 to 1.5
- bn3_bias: bfloat16 [1024], P(('dp', 'fsdp')), may hold values from -3 to 3
- w_patch: bfloat16 [1024, 768], P(('dp', 'fsdp')), may hold values from -0.1875 to 0.1875
- b_patch: bfloat16 [768], P(('dp', 'fsdp')), may hold values from -3 to 3
- ln1_gain: bfloat16 [768], P(('dp', 'fsdp')), may hold values from 0.25 to 1.75
- ln1_bias: bfloat16 [768], P(('dp', 'fsdp')), may hold values from -2 to 2
- w_qkv: bfloat16 [768, 2304], P(('dp', 'fsdp')), may hold values from -0.21875 to 0.21875
- b_qv: bfloat16 [1536], P(('dp', 'fsdp')), may hold values from -2 to 2
- w_out: bfloat16 [768, 768], P(('dp', 'fsdp')), may hold values from -0.625 to 0.625
- b_out: bfloat16 [768], P(('dp', 'fsdp')), may hold values from -2 to 2
- ln2_gain: bfloat16 [768], P(('dp', 'fsdp')), may hold values from 0.25 to 1.75
- ln2_bias: bfloat16 [768], P(('dp', 'fsdp')), may hold values from -2 to 2
- w_up: bfloat16 [768, 3072], P(('dp', 'fsdp')), may hold values from -0.21875 to 0.21875
- b_up: bfloat16 [3072], P(('dp', 'fsdp')), may hold values from -3 to 3
- w_down: bfloat16 [3072, 768], P(('dp', 'fsdp')), may hold values from -0.109375 to 0.109375
- b_down: bfloat16 [768], P(('dp', 'fsdp')), may hold values from -2 to 2
Outputs:
- output: bfloat16 [192, 260, 768], P(('dp', 'fsdp'))
- grad_feats: bfloat16 [192, 196, 1024], P(('dp', 'fsdp'))
- grad_text: bfloat16 [192, 64, 768], P(('dp', 'fsdp'))
- grad_w_red: float32 [1024, 256], P(('dp', 'fsdp'))
- grad_bn1_gain: float32 [256], P(('dp', 'fsdp'))
- grad_bn1_bias: float32 [256], P(('dp', 'fsdp'))
- grad_w_conv: float32 [2304, 256], P(('dp', 'fsdp'))
- grad_bn2_gain: float32 [256], P(('dp', 'fsdp'))
- grad_bn2_bias: float32 [256], P(('dp', 'fsdp'))
- grad_w_exp: float32 [256, 1024], P(('dp', 'fsdp'))
- grad_bn3_gain: float32 [1024], P(('dp', 'fsdp'))
- grad_bn3_bias: float32 [1024], P(('dp', 'fsdp'))
- grad_w_patch: float32 [1024, 768], P(('dp', 'fsdp'))
- grad_b_patch: float32 [768], P(('dp', 'fsdp'))
- grad_ln1_gain: float32 [768], P(('dp', 'fsdp'))
- grad_ln1_bias: float32 [768], P(('dp', 'fsdp'))
- grad_w_qkv: float32 [768, 2304], P(('dp', 'fsdp'))
- grad_b_qv: float32 [1536], P(('dp', 'fsdp'))
- grad_w_out: float32 [768, 768], P(('dp', 'fsdp'))
- grad_b_out: float32 [768], P(('dp', 'fsdp'))
- grad_ln2_gain: float32 [768], P(('dp', 'fsdp'))
- grad_ln2_bias: float32 [768], P(('dp', 'fsdp'))
- grad_w_up: float32 [768, 3072], P(('dp', 'fsdp'))
- grad_b_up: float32 [3072], P(('dp', 'fsdp'))
- grad_w_down: float32 [3072, 768], P(('dp', 'fsdp'))
- grad_b_down: float32 [768], P(('dp', 'fsdp'))
Inputs may be any that keep to these rules, and one draw needn't show every extreme that they name: `lengths`: each example has 1 to 64 text tokens; some example has 64.
All inputs are finite; a program needn't handle non-finite values.
Results may differ from a plain program's by a relative error of at most 0.019.
Values may be sent and summed in bfloat16 or wider, within the bound.
A program may use at most 320 MiB of HBM per device.

v0:
```python
import jax
import jax.numpy as jnp
from jax import lax
from jax.sharding import PartitionSpec as P

HEAD_DIM = 64
GRID = 14


ln_eps = 1e-06
bn_eps = 1e-05
gelu_coef = 0.7978845608028654


def smooth(values):
    return (
        0.5 * values * (1.0 + jnp.tanh(gelu_coef * (values + 0.044715 * values * values * values)))
    )


def normed(values, gain_vec, shift_vec):
    center = values - jnp.mean(values, -1, keepdims=True)
    return (
        center * lax.rsqrt(jnp.mean(center * center, -1, keepdims=True) + ln_eps) * gain_vec
        + shift_vec
    )


def unfold(maps):
    grid_size = maps.shape[1]
    padded = jnp.pad(maps, ((0, 0), (1, 1), (1, 1), (0, 0)))
    pieces = [
        padded[:, row_off : row_off + grid_size, col_off : col_off + grid_size, :]
        for row_off in range(3)
        for col_off in range(3)
    ]
    return jnp.concatenate(pieces, -1).reshape(-1, 9 * maps.shape[3])


def matmul(left, right):
    return jnp.dot(left, right, preferred_element_type=jnp.float32)


def left_product(left, right):
    return lax.dot_general(
        left, right, (((0,), (0,)), ((), ())), preferred_element_type=jnp.float32
    )


def right_product(left, right):
    return lax.dot_general(
        left, right, (((1,), (1,)), ((), ())), preferred_element_type=jnp.float32
    )


def batch_forward(pre_values, gain_vec, shift_vec):
    column_sum, column_squares = lax.psum(
        (jnp.sum(pre_values, 0), jnp.sum(pre_values * pre_values, 0)), ("dp", "fsdp")
    )
    total_rows = pre_values.shape[0] * lax.axis_size(("dp", "fsdp"))
    batch_mean = column_sum / total_rows
    inv_std = lax.rsqrt(column_squares / total_rows - batch_mean * batch_mean + bn_eps)
    norm_part = (pre_values - batch_mean) * inv_std
    return (
        norm_part * gain_vec.astype(jnp.float32) + shift_vec.astype(jnp.float32),
        norm_part,
        inv_std,
    )


def batch_backward(grad_shift, norm_part, inv_std, gain_vec):
    total_rows = grad_shift.shape[0] * lax.axis_size(("dp", "fsdp"))
    total_bias, total_gain = lax.psum(
        (jnp.sum(grad_shift, 0), jnp.sum(grad_shift * norm_part, 0)), ("dp", "fsdp")
    )
    grad_pre = (
        inv_std
        * gain_vec.astype(jnp.float32)
        * (grad_shift - total_bias / total_rows - norm_part * total_gain / total_rows)
    )
    return (grad_pre.astype(jnp.bfloat16), total_gain, total_bias)


def own_share(whole, share):
    return lax.dynamic_slice_in_dim(whole, lax.axis_index(("dp", "fsdp")) * share, share, 0)


def smooth_grad(point, grad_out):
    _, smooth_back = jax.vjp(smooth, point)
    return smooth_back(grad_out)[0]


def forward_pass(feats, text, lengths, weights):
    (
        w_red,
        bn1_gain,
        bn1_bias,
        w_conv,
        bn2_gain,
        bn2_bias,
        w_exp,
        bn3_gain,
        bn3_bias,
        w_patch,
        b_patch,
        ln1_gain,
        ln1_bias,
        w_qkv,
        b_qv,
        w_out,
        b_out,
        ln2_gain,
        ln2_bias,
        w_up,
        b_up,
        w_down,
        b_down,
    ) = weights
    examples, patches, channels = feats.shape
    grid_size = GRID
    bottleneck = w_red.shape[1]
    text_slots = text.shape[1]
    model_width = text.shape[2]
    head_count = model_width // HEAD_DIM
    seq_len = patches + text_slots
    feat_rows = feats.reshape(-1, channels)
    red_pre = matmul(feat_rows, w_red)
    red_shift, red_norm, red_inv = batch_forward(red_pre, bn1_gain, bn1_bias)
    red_act = smooth(red_shift).astype(jnp.bfloat16)
    columns = unfold(red_act.reshape(examples, grid_size, grid_size, bottleneck))
    conv_pre = matmul(columns, w_conv)
    conv_shift, conv_norm, conv_inv = batch_forward(conv_pre, bn2_gain, bn2_bias)
    conv_act = smooth(conv_shift).astype(jnp.bfloat16)
    expand_pre = matmul(conv_act, w_exp)
    expand_shift, expand_norm, expand_inv = batch_forward(expand_pre, bn3_gain, bn3_bias)
    joined = expand_shift + feat_rows.astype(jnp.float32)
    stem_act = smooth(joined).astype(jnp.bfloat16)
    patch = matmul(stem_act, w_patch) + b_patch.astype(jnp.float32)
    keep = (jnp.arange(text_slots, dtype=jnp.int32)[None, :] < lengths[:, None]).astype(jnp.float32)
    valid = jnp.concatenate([jnp.ones((examples, patches), jnp.float32), keep], 1)
    stream = jnp.concatenate(
        [
            patch.reshape(examples, patches, model_width),
            text.astype(jnp.float32) * keep[:, :, None],
        ],
        1,
    ).reshape(-1, model_width)
    first_norm = normed(stream, ln1_gain.astype(jnp.float32), ln1_bias.astype(jnp.float32)).astype(
        jnp.bfloat16
    )
    qkv_bias = jnp.concatenate(
        [b_qv[:model_width], jnp.zeros((model_width,), jnp.bfloat16), b_qv[model_width:]]
    ).astype(jnp.float32)
    qkv = (matmul(first_norm, w_qkv) + qkv_bias).astype(jnp.bfloat16)
    qkv = qkv.reshape(examples, seq_len, 3, head_count, HEAD_DIM)
    query = qkv[:, :, 0]
    key_part = qkv[:, :, 1]
    value_part = qkv[:, :, 2]
    scores = jnp.einsum(
        "eqhd,ekhd->ehqk", query, key_part, preferred_element_type=jnp.float32
    ) * HEAD_DIM ** (-0.5)
    scores = jnp.where(valid[:, None, None, :] > 0.5, scores, -1e30)
    top_score = jnp.max(scores, -1, keepdims=True)
    expo_scores = jnp.exp(scores - top_score)
    probs = expo_scores / jnp.sum(expo_scores, -1, keepdims=True)
    probs_low = probs.astype(jnp.bfloat16)
    mixed = jnp.einsum("ehqk,ekhd->eqhd", probs_low, value_part, preferred_element_type=jnp.float32)
    mixed = mixed.astype(jnp.bfloat16).reshape(-1, model_width)
    second = stream + matmul(mixed, w_out) + b_out.astype(jnp.float32)
    second_norm = normed(second, ln2_gain.astype(jnp.float32), ln2_bias.astype(jnp.float32)).astype(
        jnp.bfloat16
    )
    upper = matmul(second_norm, w_up) + b_up.astype(jnp.float32)
    hidden = smooth(upper).astype(jnp.bfloat16)
    result = second + matmul(hidden, w_down) + b_down.astype(jnp.float32)
    output = (result.reshape(examples, seq_len, model_width) * valid[:, :, None]).astype(
        jnp.bfloat16
    )
    saved = dict(
        feat_rows=feat_rows,
        red_shift=red_shift,
        red_norm=red_norm,
        red_inv=red_inv,
        red_act=red_act,
        columns=columns,
        conv_shift=conv_shift,
        conv_norm=conv_norm,
        conv_inv=conv_inv,
        conv_act=conv_act,
        expand_norm=expand_norm,
        expand_inv=expand_inv,
        joined=joined,
        stem_act=stem_act,
        keep=keep,
        valid=valid,
        stream=stream,
        first_norm=first_norm,
        query=query,
        key_part=key_part,
        value_part=value_part,
        probs=probs,
        probs_low=probs_low,
        mixed=mixed,
        second=second,
        second_norm=second_norm,
        upper=upper,
        hidden=hidden,
    )
    return (output, saved)


def local(
    feats,
    text,
    lengths,
    cotangent,
    w_red,
    bn1_gain,
    bn1_bias,
    w_conv,
    bn2_gain,
    bn2_bias,
    w_exp,
    bn3_gain,
    bn3_bias,
    w_patch,
    b_patch,
    ln1_gain,
    ln1_bias,
    w_qkv,
    b_qv,
    w_out,
    b_out,
    ln2_gain,
    ln2_bias,
    w_up,
    b_up,
    w_down,
    b_down,
):
    gathered = (
        lax.all_gather(w_red, ("dp", "fsdp"), axis=0, tiled=True),
        lax.all_gather(bn1_gain, ("dp", "fsdp"), axis=0, tiled=True),
        lax.all_gather(bn1_bias, ("dp", "fsdp"), axis=0, tiled=True),
        lax.all_gather(w_conv, ("dp", "fsdp"), axis=0, tiled=True),
        lax.all_gather(bn2_gain, ("dp", "fsdp"), axis=0, tiled=True),
        lax.all_gather(bn2_bias, ("dp", "fsdp"), axis=0, tiled=True),
        lax.all_gather(w_exp, ("dp", "fsdp"), axis=0, tiled=True),
        lax.all_gather(bn3_gain, ("dp", "fsdp"), axis=0, tiled=True),
        lax.all_gather(bn3_bias, ("dp", "fsdp"), axis=0, tiled=True),
        lax.all_gather(w_patch, ("dp", "fsdp"), axis=0, tiled=True),
        lax.all_gather(b_patch, ("dp", "fsdp"), axis=0, tiled=True),
        lax.all_gather(ln1_gain, ("dp", "fsdp"), axis=0, tiled=True),
        lax.all_gather(ln1_bias, ("dp", "fsdp"), axis=0, tiled=True),
        lax.all_gather(w_qkv, ("dp", "fsdp"), axis=0, tiled=True),
        lax.all_gather(b_qv, ("dp", "fsdp"), axis=0, tiled=True),
        lax.all_gather(w_out, ("dp", "fsdp"), axis=0, tiled=True),
        lax.all_gather(b_out, ("dp", "fsdp"), axis=0, tiled=True),
        lax.all_gather(ln2_gain, ("dp", "fsdp"), axis=0, tiled=True),
        lax.all_gather(ln2_bias, ("dp", "fsdp"), axis=0, tiled=True),
        lax.all_gather(w_up, ("dp", "fsdp"), axis=0, tiled=True),
        lax.all_gather(b_up, ("dp", "fsdp"), axis=0, tiled=True),
        lax.all_gather(w_down, ("dp", "fsdp"), axis=0, tiled=True),
        lax.all_gather(b_down, ("dp", "fsdp"), axis=0, tiled=True),
    )
    output, saved = forward_pass(feats, text, lengths, gathered)
    weights = (
        lax.all_gather(w_red, ("dp", "fsdp"), axis=0, tiled=True),
        lax.all_gather(bn1_gain, ("dp", "fsdp"), axis=0, tiled=True),
        lax.all_gather(bn1_bias, ("dp", "fsdp"), axis=0, tiled=True),
        lax.all_gather(w_conv, ("dp", "fsdp"), axis=0, tiled=True),
        lax.all_gather(bn2_gain, ("dp", "fsdp"), axis=0, tiled=True),
        lax.all_gather(bn2_bias, ("dp", "fsdp"), axis=0, tiled=True),
        lax.all_gather(w_exp, ("dp", "fsdp"), axis=0, tiled=True),
        lax.all_gather(bn3_gain, ("dp", "fsdp"), axis=0, tiled=True),
        lax.all_gather(bn3_bias, ("dp", "fsdp"), axis=0, tiled=True),
        lax.all_gather(w_patch, ("dp", "fsdp"), axis=0, tiled=True),
        lax.all_gather(b_patch, ("dp", "fsdp"), axis=0, tiled=True),
        lax.all_gather(ln1_gain, ("dp", "fsdp"), axis=0, tiled=True),
        lax.all_gather(ln1_bias, ("dp", "fsdp"), axis=0, tiled=True),
        lax.all_gather(w_qkv, ("dp", "fsdp"), axis=0, tiled=True),
        lax.all_gather(b_qv, ("dp", "fsdp"), axis=0, tiled=True),
        lax.all_gather(w_out, ("dp", "fsdp"), axis=0, tiled=True),
        lax.all_gather(b_out, ("dp", "fsdp"), axis=0, tiled=True),
        lax.all_gather(ln2_gain, ("dp", "fsdp"), axis=0, tiled=True),
        lax.all_gather(ln2_bias, ("dp", "fsdp"), axis=0, tiled=True),
        lax.all_gather(w_up, ("dp", "fsdp"), axis=0, tiled=True),
        lax.all_gather(b_up, ("dp", "fsdp"), axis=0, tiled=True),
        lax.all_gather(w_down, ("dp", "fsdp"), axis=0, tiled=True),
        lax.all_gather(b_down, ("dp", "fsdp"), axis=0, tiled=True),
    )
    (
        full_red,
        full_bn1_gain,
        full_bn1_bias,
        full_conv,
        full_bn2_gain,
        full_bn2_bias,
        full_exp,
        full_bn3_gain,
        full_bn3_bias,
        full_patch,
        full_b_patch,
        full_ln1_gain,
        full_ln1_bias,
        full_qkv,
        full_b_qv,
        full_out,
        full_b_out,
        full_ln2_gain,
        full_ln2_bias,
        full_up,
        full_b_up,
        full_down,
        full_b_down,
    ) = weights
    examples, patches, channels = feats.shape
    bottleneck = w_red.shape[1]
    model_width = text.shape[2]
    head_count = model_width // HEAD_DIM
    seq_len = cotangent.shape[1]
    scale_factor = HEAD_DIM ** (-0.5)
    grad_rows = (cotangent.astype(jnp.float32) * saved["valid"][:, :, None]).reshape(
        -1, model_width
    )
    grad_low = grad_rows.astype(jnp.bfloat16)
    g_down = left_product(saved["hidden"], grad_low)
    g_b_down = jnp.sum(grad_rows, 0)
    g_hidden = right_product(grad_low, full_down)
    g_upper = smooth_grad(saved["upper"], g_hidden).astype(jnp.bfloat16)
    g_up = left_product(saved["second_norm"], g_upper)
    g_b_up = jnp.sum(g_upper.astype(jnp.float32), 0)
    g_second_norm = right_product(g_upper, full_up)
    _, norm_back = jax.vjp(
        normed,
        saved["second"],
        full_ln2_gain.astype(jnp.float32),
        full_ln2_bias.astype(jnp.float32),
    )
    g_second, g_ln2_gain, g_ln2_bias = norm_back(g_second_norm)
    g_second = g_second + grad_rows
    g_branch = g_second.astype(jnp.bfloat16)
    g_out = left_product(saved["mixed"], g_branch)
    g_b_out = jnp.sum(g_branch.astype(jnp.float32), 0)
    g_mixed = (
        right_product(g_branch, full_out)
        .astype(jnp.bfloat16)
        .reshape(examples, seq_len, head_count, HEAD_DIM)
    )
    g_value = jnp.einsum(
        "ehqk,eqhd->ekhd", saved["probs_low"], g_mixed, preferred_element_type=jnp.float32
    )
    g_probs = jnp.einsum(
        "eqhd,ekhd->ehqk", g_mixed, saved["value_part"], preferred_element_type=jnp.float32
    )
    probs = saved["probs"]
    g_scores = (probs * (g_probs - jnp.sum(probs * g_probs, -1, keepdims=True))).astype(
        jnp.bfloat16
    )
    g_query = (
        jnp.einsum(
            "ehqk,ekhd->eqhd", g_scores, saved["key_part"], preferred_element_type=jnp.float32
        )
        * scale_factor
    )
    g_key = (
        jnp.einsum("ehqk,eqhd->ekhd", g_scores, saved["query"], preferred_element_type=jnp.float32)
        * scale_factor
    )
    g_qkv_rows = (
        jnp.stack([g_query, g_key, g_value], 2).astype(jnp.bfloat16).reshape(-1, 3 * model_width)
    )
    g_qkv = left_product(saved["first_norm"], g_qkv_rows)
    qkv_sums = jnp.sum(g_qkv_rows.astype(jnp.float32), 0)
    g_b_qv = jnp.concatenate([qkv_sums[:model_width], qkv_sums[2 * model_width :]])
    g_first_norm = right_product(g_qkv_rows, full_qkv)
    _, first_back = jax.vjp(
        normed,
        saved["stream"],
        full_ln1_gain.astype(jnp.float32),
        full_ln1_bias.astype(jnp.float32),
    )
    g_stream, g_ln1_gain, g_ln1_bias = first_back(g_first_norm)
    g_stream = (g_stream + g_second).reshape(examples, seq_len, model_width)
    grad_text = (g_stream[:, patches:] * saved["keep"][:, :, None]).astype(jnp.bfloat16)
    g_patch_rows = g_stream[:, :patches].reshape(-1, model_width).astype(jnp.bfloat16)
    g_patch = left_product(saved["stem_act"], g_patch_rows)
    g_b_patch = jnp.sum(g_patch_rows.astype(jnp.float32), 0)
    g_act = right_product(g_patch_rows, full_patch)
    g_joined = smooth_grad(saved["joined"], g_act)
    g_expand_low, t_bn3_gain, t_bn3_bias = batch_backward(
        g_joined, saved["expand_norm"], saved["expand_inv"], full_bn3_gain
    )
    g_exp = left_product(saved["conv_act"], g_expand_low)
    g_conv_act = right_product(g_expand_low, full_exp)
    g_conv_shift = smooth_grad(saved["conv_shift"], g_conv_act)
    g_conv_low, t_bn2_gain, t_bn2_bias = batch_backward(
        g_conv_shift, saved["conv_norm"], saved["conv_inv"], full_bn2_gain
    )
    g_conv = left_product(saved["columns"], g_conv_low)
    g_columns = right_product(g_conv_low, full_conv)
    _, fold_back = jax.vjp(unfold, jnp.zeros((examples, GRID, GRID, bottleneck), jnp.float32))
    g_red_act = fold_back(g_columns)[0].reshape(-1, bottleneck)
    g_red_shift = smooth_grad(saved["red_shift"], g_red_act)
    g_red_low, t_bn1_gain, t_bn1_bias = batch_backward(
        g_red_shift, saved["red_norm"], saved["red_inv"], full_bn1_gain
    )
    g_red = left_product(saved["feat_rows"], g_red_low)
    grad_feats = (
        (g_joined + right_product(g_red_low, full_red))
        .astype(jnp.bfloat16)
        .reshape(examples, patches, channels)
    )
    shares = (
        lax.psum_scatter(g_red, ("dp", "fsdp"), scatter_dimension=0, tiled=True),
        lax.psum_scatter(g_conv, ("dp", "fsdp"), scatter_dimension=0, tiled=True),
        lax.psum_scatter(g_exp, ("dp", "fsdp"), scatter_dimension=0, tiled=True),
        lax.psum_scatter(g_patch, ("dp", "fsdp"), scatter_dimension=0, tiled=True),
        lax.psum_scatter(g_b_patch, ("dp", "fsdp"), scatter_dimension=0, tiled=True),
        lax.psum_scatter(g_ln1_gain, ("dp", "fsdp"), scatter_dimension=0, tiled=True),
        lax.psum_scatter(g_ln1_bias, ("dp", "fsdp"), scatter_dimension=0, tiled=True),
        lax.psum_scatter(g_qkv, ("dp", "fsdp"), scatter_dimension=0, tiled=True),
        lax.psum_scatter(g_b_qv, ("dp", "fsdp"), scatter_dimension=0, tiled=True),
        lax.psum_scatter(g_out, ("dp", "fsdp"), scatter_dimension=0, tiled=True),
        lax.psum_scatter(g_b_out, ("dp", "fsdp"), scatter_dimension=0, tiled=True),
        lax.psum_scatter(g_ln2_gain, ("dp", "fsdp"), scatter_dimension=0, tiled=True),
        lax.psum_scatter(g_ln2_bias, ("dp", "fsdp"), scatter_dimension=0, tiled=True),
        lax.psum_scatter(g_up, ("dp", "fsdp"), scatter_dimension=0, tiled=True),
        lax.psum_scatter(g_b_up, ("dp", "fsdp"), scatter_dimension=0, tiled=True),
        lax.psum_scatter(g_down, ("dp", "fsdp"), scatter_dimension=0, tiled=True),
        lax.psum_scatter(g_b_down, ("dp", "fsdp"), scatter_dimension=0, tiled=True),
    )
    s_red, s_conv, s_exp, s_patch, s_b_patch = shares[:5]
    block_shares = shares[5:]
    (
        s_ln1_gain,
        s_ln1_bias,
        s_qkv,
        s_b_qv,
        s_out,
        s_b_out,
        s_ln2_gain,
        s_ln2_bias,
        s_up,
        s_b_up,
        s_down,
        s_b_down,
    ) = block_shares
    narrow = bn1_gain.shape[0]
    broad = bn3_gain.shape[0]
    return (
        output,
        grad_feats,
        grad_text,
        s_red,
        own_share(t_bn1_gain, narrow),
        own_share(t_bn1_bias, narrow),
        s_conv,
        own_share(t_bn2_gain, narrow),
        own_share(t_bn2_bias, narrow),
        s_exp,
        own_share(t_bn3_gain, broad),
        own_share(t_bn3_bias, broad),
        s_patch,
        s_b_patch,
        s_ln1_gain,
        s_ln1_bias,
        s_qkv,
        s_b_qv,
        s_out,
        s_b_out,
        s_ln2_gain,
        s_ln2_bias,
        s_up,
        s_b_up,
        s_down,
        s_b_down,
    )


def solution(mesh):
    return jax.shard_map(
        local,
        mesh=mesh,
        in_specs=(
            P(("dp", "fsdp"), None, None),
            P(("dp", "fsdp"), None, None),
            P(("dp", "fsdp")),
            P(("dp", "fsdp"), None, None),
            P(("dp", "fsdp"), None),
            P(("dp", "fsdp")),
            P(("dp", "fsdp")),
            P(("dp", "fsdp"), None),
            P(("dp", "fsdp")),
            P(("dp", "fsdp")),
            P(("dp", "fsdp"), None),
            P(("dp", "fsdp")),
            P(("dp", "fsdp")),
            P(("dp", "fsdp"), None),
            P(("dp", "fsdp")),
            P(("dp", "fsdp")),
            P(("dp", "fsdp")),
            P(("dp", "fsdp"), None),
            P(("dp", "fsdp")),
            P(("dp", "fsdp"), None),
            P(("dp", "fsdp")),
            P(("dp", "fsdp")),
            P(("dp", "fsdp")),
            P(("dp", "fsdp"), None),
            P(("dp", "fsdp")),
            P(("dp", "fsdp"), None),
            P(("dp", "fsdp")),
        ),
        out_specs=(
            P(("dp", "fsdp"), None, None),
            P(("dp", "fsdp"), None, None),
            P(("dp", "fsdp"), None, None),
            P(("dp", "fsdp"), None),
            P(("dp", "fsdp")),
            P(("dp", "fsdp")),
            P(("dp", "fsdp"), None),
            P(("dp", "fsdp")),
            P(("dp", "fsdp")),
            P(("dp", "fsdp"), None),
            P(("dp", "fsdp")),
            P(("dp", "fsdp")),
            P(("dp", "fsdp"), None),
            P(("dp", "fsdp")),
            P(("dp", "fsdp")),
            P(("dp", "fsdp")),
            P(("dp", "fsdp"), None),
            P(("dp", "fsdp")),
            P(("dp", "fsdp"), None),
            P(("dp", "fsdp")),
            P(("dp", "fsdp")),
            P(("dp", "fsdp")),
            P(("dp", "fsdp"), None),
            P(("dp", "fsdp")),
            P(("dp", "fsdp"), None),
            P(("dp", "fsdp")),
        ),
        check_vma=False,
    )
```

profile of v0, /device:TPU:0, one launch (start us, length us, event | category | flops | bytes accessed | tf_op | source)
XLA Modules:
  0.0 1844.7 jit_solution(9742834485515381622)
XLA Ops:
  15.5 45.7 %all_gather.82 = bf16[1024,256]{1,0:T(8,128)(2,1)S(1)} all-gather(bf16[32,256]{1,0:T(8,128)(2,1)S(1)} %copy-done.66), channel_id=1, replica_groups=mesh['dp'=4,'fsdp'=8] {'dp','fsdp'}, dimensions={0}, use_global_device_ids=true | all-gather | bytes 540672 | tf_op jit(solution)/shard_map/all_gather | solution.py:242
  64.8 37.6 %all-reduce.41 = (bf16[1024]{0:T(1024)(128)(2,1)S(1)}, bf16[1024]{0:T(1024)(128)(2,1)S(1)}, bf16[256]{0:T(256)(128)(2,1)S(1)}, bf16[256]{0:T(256)(128)(2,1)S(1)}...) all-reduce(bf16[1024]{0:T(1024)(128)(2,1)S(1)} %dynamic-update-slic, ...), channel_id=1, replica_groups=mesh['dp'=4,'fsdp'=8] {'dp','fsdp'}, use_global_device_ids=true, to_apply=%add.16 | all-reduce | flops 13056 | bytes 52224
  105.0 41.1 %all-reduce.40 = (f32[256]{0:T(256)S(1)}, f32[256]{0:T(256)S(1)}) all-reduce(f32[256]{0:T(256)S(1)} %get-tuple-element.121, f32[256]{0:T(256)S(1)} %get-tuple-element.120), channel_id=1, replica_groups=mesh['dp'=4,'fsdp'=8] {'dp','fsdp'}, use_global_device_ids=true, to_apply=%region_3.0 | all-reduce | flops 512 | bytes 4096 | tf_op jit(solution)/shard_map/psum | solution.py:57
  174.8 46.8 %all_gather.88 = bf16[256,1024]{1,0:T(8,128)(2,1)} all-gather(bf16[8,1024]{1,0:T(8,128)(2,1)S(1)} %copy-done.67), channel_id=1, replica_groups=mesh['dp'=4,'fsdp'=8] {'dp','fsdp'}, dimensions={0}, use_global_device_ids=true | all-gather | bytes 540672 | tf_op jit(solution)/shard_map/all_gather | solution.py:248
  236.5 37.4 %all-reduce.39 = (f32[256]{0:T(256)S(1)}, f32[256]{0:T(256)S(1)}) all-reduce(f32[256]{0:T(256)S(1)} %get-tuple-element.119, f32[256]{0:T(256)S(1)} %get-tuple-element.118), channel_id=1, replica_groups=mesh['dp'=4,'fsdp'=8] {'dp','fsdp'}, use_global_device_ids=true, to_apply=%region_7.8 | all-reduce | flops 512 | bytes 4096 | tf_op jit(solution)/shard_map/psum | solution.py:57
  277.8 41.6 %all-reduce.38 = (f32[1024]{0:T(1024)S(1)}, f32[1024]{0:T(1024)S(1)}) all-reduce(f32[1024]{0:T(1024)S(1)} %get-tuple-element.111, f32[1024]{0:T(1024)S(1)} %get-tuple-element.110), channel_id=1, replica_groups=mesh['dp'=4,'fsdp'=8] {'dp','fsdp'}, use_global_device_ids=true, to_apply=%region_11.12 | all-reduce | flops 2048 | bytes 16384 | tf_op jit(solution)/shard_map/psum | solution.py:57
  363.0 22.4 %reshape.402 = bf16[6,260,3,12,64]{4,3,2,1,0:T(8,128)(2,1)} reshape(bf16[1560,2304]{1,0:T(8,128)(2,1)} %add_convert_fusion) | data formatting | bytes 14376960 | tf_op jit(solution)/shard_map/reshape | solution.py:155
  385.4 14.4 fusion.86
  428.3 15.4 fusion.22
  443.8 37.3 %fusion.90 = (f32[6,12,260]{2,1,0:T(8,128)}, f32[6,12,260,260]{2,3,1,0:T(8,128)}) fusion(f32[6,12,260,260]{2,3,1,0:T(8,128)} %fusion.22, pred[6,260]{1,0:T(8,128)(4,1)S(1)} %broadcast_compare_fusion), kind=kOutput, calls=%fused_computation.195 | output fusion | flops 29203460 | bytes 39014040 | tf_op jit(solution)/shard_map/sub | solution.py:164
  512.0 15.4 fusion.72
  527.4 19.4 %add_add_fusion.4 = f32[1560,768]{1,0:T(8,128)} fusion(f32[1560,768]{1,0:T(8,128)} %copy-done.8, bf16[3072,768]{1,0:T(8,128)(2,1)} %all-gather.17.cloned.1.call-done, f32[768]{0:T(1024)S(1)} %copy-done.85, f32[1560,3072]{1,0:T(8,128)} %fusion.72, f32[3072]{0:T(1024)S(1)} %copy-done.68), kind=kOutput, calls=%fused_computation.61 | convolution fusion | flops 7411322880 | bytes 33487872 | tf_op jit(solution)/shard_map/dot_general | solution.py:41
  564.9 30.5 %convert_reduce_fusion.1 = (f32[3072]{0:T(1024)}, bf16[1560,3072]{1,0:T(8,128)(2,1)}) fusion(bf16[3072,768]{1,0:T(8,128)(2,1)} %all-gather.17.cloned.1.call-done, f32[1560,768]{1,0:T(8,128)} %reshape.364, f32[1560,3072]{1,0:T(8,128)} %fusion.72, f32[3072]{0:T(1024)S(1)} %copy-done.68), kind=kOutput, calls=%fused_computation.18 | convolution fusion | flops 7491591168 | bytes 38289408 | tf_op jit(solution)/shard_map/dot_general | solution.py:51
  595.4 14.7 multiply_reduce_fusion.4
  633.1 23.8 %multiply_reduce_fusion = (f32[6,12,260]{2,1,0:T(8,128)}, f32[6,12,260,260]{2,3,1,0:T(8,128)}) fusion(f32[6,12,260,260]{2,3,1,0:T(8,128)} %get-tuple-element.215, f32[6,12,260]{2,1,0:T(8,128)} %get-tuple-element.214, bf16[6,260,12,64]{1,3,2,0:T(8,128)(2,1)} %copy.84, bf16[6,260,1,12,64]{1,4,3,0,2:T(8,128)(2,1)S(1)} %copy-done.16), kind=kOutput, calls=%fused_computation.2 | convolution fusion | flops 637584512 | bytes 43879680 | tf_op jit(solution)/shard_map/eqhd,ekhd->ehqk/dot_general | solution.py:353
  656.8 24.4 %multiply_convert_fusion = bf16[6,12,260,260]{2,3,1,0:T(8,128)(2,1)} fusion(f32[6,12,260,260]{2,3,1,0:T(8,128)} %get-tuple-element.220, f32[6,12,260]{2,1,0:T(8,128)} %get-tuple-element.219, f32[6,12,260,260]{2,3,1,0:T(8,128)} %get-tuple-element.215, f32[6,12,260]{2,1,0:T(8,128)} %get-tuple-element.214), kind=kLoop, calls=%fused_computation.1 | loop fusion | flops 19468800 | bytes 48821760 | tf_op jit(solution)/shard_map/convert_element_type | solution.py:357
  698.2 15.1 fusion.30
  731.0 19.4 %convert_element_type.218 = bf16[1560,2304]{0,1:T(8,128)(2,1)} reshape(bf16[6,260,3,12,64]{1,0,4,3,2:T(8,128)(2,1)} %copy.89) | data formatting | bytes 14376960 | tf_op jit(solution)/shard_map/convert_element_type | solution.py:371
  750.4 14.1 multiply_reduce_fusion.5
  797.6 40.4 %all-reduce.37 = (f32[1024]{0:T(1024)S(1)}, f32[1024]{0:T(1024)S(1)}) all-reduce(f32[1024]{0:T(1024)S(1)} %get-tuple-element.109, f32[1024]{0:T(1024)S(1)} %get-tuple-element.108), channel_id=1, replica_groups=mesh['dp'=4,'fsdp'=8] {'dp','fsdp'}, use_global_device_ids=true, to_apply=%region_26.27 | all-reduce | flops 2048 | bytes 16384 | tf_op jit(solution)/shard_map/psum | solution.py:73
  849.8 39.9 %all-reduce.36 = (f32[256]{0:T(256)S(1)}, f32[256]{0:T(256)S(1)}) all-reduce(f32[256]{0:T(256)S(1)} %get-tuple-element.117, f32[256]{0:T(256)S(1)} %get-tuple-element.116), channel_id=1, replica_groups=mesh['dp'=4,'fsdp'=8] {'dp','fsdp'}, use_global_device_ids=true, to_apply=%region_30.31 | all-reduce | flops 512 | bytes 4096 | tf_op jit(solution)/shard_map/psum | solution.py:73
  897.4 12.6 reshape.367
  928.5 42.2 %all-reduce.35 = (f32[256]{0:T(256)S(1)}, f32[256]{0:T(256)S(1)}, f32[768]{0:T(1024)}, f32[768]{0:T(1024)}, f32[768]{0:T(1024)}, /*index=5*/f32[1536]{0:T(1024)}...) all-reduce(f32[256]{0:T(256)S(1)} %get-tuple-element.115, ...), channel_id=1, replica_groups=mesh['dp'=4,'fsdp'=8] {'dp','fsdp'}, use_global_device_ids=true, to_apply=%region_34.35 | all-reduce | flops 10496 | bytes 83968 | tf_op jit(solution)/shard_map/psum | solution.py:73
  1012.3 20.0 %fusion.55 = f32[3072,768]{1,0:T(8,128)} fusion(f32[1560,768]{1,0:T(8,128)} %reshape.364, f32[1560,3072]{1,0:T(8,128)} %fusion.72, f32[3072]{0:T(1024)S(1)} %copy-done.69), kind=kOutput, calls=%fused_computation.124 | convolution fusion | flops 7410124800 | bytes 33411072 | tf_op jit(solution)/shard_map/dot_general | solution.py:45
  1033.0 15.8 fusion.71
  1071.4 46.9 %reduce-scatter.25.cloned.1.call-done = f32[32,256]{1,0:T(8,128)} async-done(((f32[1024,256]{1,0:T(8,128)}), f32[32,256]{1,0:T(8,128)}) %reduce-scatter.25.cloned.1.call-update) | async-done | bytes 32784
  1118.3 101.1 %reduce-scatter.19.cloned.1.call-done = f32[24,768]{1,0:T(8,128)} async-done(((f32[768,768]{1,0:T(8,128)}), f32[24,768]{1,0:T(8,128)}) %reduce-scatter.19.cloned.1.call-update) | async-done | bytes 73744 | tf_op jit(solution)/shard_map/reduce_scatter | solution.py:424
  1219.5 104.6 %reduce-scatter.11.cloned.1.call-done = f32[72,256]{1,0:T(8,128)} async-done(((f32[2304,256]{1,0:T(8,128)}), f32[72,256]{1,0:T(8,128)}) %reduce-scatter.11.cloned.1.call-update) | async-done | bytes 73744 | tf_op jit(solution)/shard_map/reduce_scatter | solution.py:416
  1324.0 106.6 %reduce-scatter.15.cloned.1.call-done = f32[32,768]{1,0:T(8,128)} async-done(((f32[1024,768]{1,0:T(8,128)}), f32[32,768]{1,0:T(8,128)}) %reduce-scatter.15.cloned.1.call-update) | async-done | bytes 98320 | tf_op jit(solution)/shard_map/reduce_scatter | solution.py:418
  1430.7 124.3 %reduce-scatter.17.cloned.1.call-done = f32[24,2304]{1,0:T(8,128)} async-done(((f32[768,2304]{1,0:T(8,128)}), f32[24,2304]{1,0:T(8,128)}) %reduce-scatter.17.cloned.1.call-update) | async-done | bytes 221200 | tf_op jit(solution)/shard_map/reduce_scatter | solution.py:422
  1554.9 142.3 %reduce-scatter.23.cloned.1.call-done = f32[96,768]{1,0:T(8,128)} async-done(((f32[3072,768]{1,0:T(8,128)}), f32[96,768]{1,0:T(8,128)}) %reduce-scatter.23.cloned.1.call-update) | async-done | bytes 294928 | tf_op jit(solution)/shard_map/reduce_scatter | solution.py:430
  1697.3 140.7 %reduce-scatter.21.cloned.1.call-done = f32[24,3072]{1,0:T(8,128)} async-done(((f32[768,3072]{1,0:T(8,128)}), f32[24,3072]{1,0:T(8,128)}) %reduce-scatter.21.cloned.1.call-update) | async-done | bytes 294928 | tf_op jit(solution)/shard_map/reduce_scatter | solution.py:428
  (429 shorter events, 375.4 us)
Async XLA Ops:
  7.3 55.8 %copy-start.98 = (bf16[8]{0:T(256)(128)(2,1)S(1)}, bf16[8]{0:T(256)(128)(2,1)}, u32[]{:S(2)}) copy-start(bf16[8]{0:T(256)(128)(2,1)} %param.33) | copy-start | bytes 52
  7.3 56.0 %copy-start.99 = (bf16[8]{0:T(256)(128)(2,1)S(1)}, bf16[8]{0:T(256)(128)(2,1)}, u32[]{:S(2)}) copy-start(bf16[8]{0:T(256)(128)(2,1)} %param.35) | copy-start | bytes 52
  7.3 56.3 %copy-start.100 = (bf16[8]{0:T(256)(128)(2,1)S(1)}, bf16[8]{0:T(256)(128)(2,1)}, u32[]{:S(2)}) copy-start(bf16[8]{0:T(256)(128)(2,1)} %param.36) | copy-start | bytes 52
  7.3 56.5 %copy-start.101 = (bf16[32]{0:T(256)(128)(2,1)S(1)}, bf16[32]{0:T(256)(128)(2,1)}, u32[]{:S(2)}) copy-start(bf16[32]{0:T(256)(128)(2,1)} %param.38) | copy-start | bytes 196
  7.3 56.7 %copy-start.102 = (bf16[32]{0:T(256)(128)(2,1)S(1)}, bf16[32]{0:T(256)(128)(2,1)}, u32[]{:S(2)}) copy-start(bf16[32]{0:T(256)(128)(2,1)} %param.39) | copy-start | bytes 196
  7.4 56.9 %copy-start.103 = (bf16[96]{0:T(256)(128)(2,1)S(1)}, bf16[96]{0:T(256)(128)(2,1)}, u32[]{:S(2)}) copy-start(bf16[96]{0:T(256)(128)(2,1)} %param.51) | copy-start | bytes 580
  7.4 57.2 %copy-start.104 = (bf16[48]{0:T(256)(128)(2,1)S(1)}, bf16[48]{0:T(256)(128)(2,1)}, u32[]{:S(2)}) copy-start(bf16[48]{0:T(256)(128)(2,1)} %param.45) | copy-start | bytes 292
  7.4 224.5 %all-gather.7.cloned.1.call-start = ((), (), s32[]{:S(2)}) async-start(), calls=%async_computation.8 | async-start | bytes 1216512 | tf_op jit(solution)/shard_map/all_gather | solution.py:245
  8.1 317.6 %all-gather.9.cloned.1.call-start = ((), (), s32[]{:S(2)}) async-start(), calls=%async_computation.9 | async-start | bytes 1622016 | tf_op jit(solution)/shard_map/all_gather | solution.py:251
  8.9 343.0 %all-gather.11.cloned.1.call-start = ((), (), s32[]{:S(2)}) async-start(), calls=%async_computation.10 | async-start | bytes 3649536 | tf_op jit(solution)/shard_map/all_gather | solution.py:255
  9.6 493.6 %all-gather.13.cloned.1.call-start = ((), (), s32[]{:S(2)}) async-start(), calls=%async_computation.11 | async-start | bytes 1216512 | tf_op jit(solution)/shard_map/all_gather | solution.py:257
  10.2 501.8 %all-gather.15.cloned.1.call-start = ((), (), s32[]{:S(2)}) async-start(), calls=%async_computation.12 | async-start | bytes 4866048 | tf_op jit(solution)/shard_map/all_gather | solution.py:261
  10.8 516.6 %all-gather.17.cloned.1.call-start = ((), (), s32[]{:S(2)}) async-start(), calls=%async_computation.13 | async-start | bytes 4866048 | tf_op jit(solution)/shard_map/all_gather | solution.py:263
  11.3 1060.1 %reduce-scatter.13.cloned.1.call-start = ((), (), s32[]{:S(2)}) async-start(), calls=%async_computation.15 | async-start | bytes 1081344 | tf_op jit(solution)/shard_map/reduce_scatter | solution.py:417
  61.2 85.5 %copy-start.24 = (bf16[1024,256]{1,0:T(8,128)(2,1)}, bf16[1024,256]{1,0:T(8,128)(2,1)S(1)}, u32[]{:S(2)}) copy-start(bf16[1024,256]{1,0:T(8,128)(2,1)S(1)} %all_gather.82) | copy-start | bytes 1572868
  102.5 67.5 %copy-start.71 = (f32[256]{0:T(256)}, f32[256]{0:T(256)S(1)}, u32[]{:S(2)}) copy-start(f32[256]{0:T(256)S(1)} %convert_element_type.182) | copy-start | bytes 3076
  102.5 67.5 %copy-start.73 = (f32[256]{0:T(256)}, f32[256]{0:T(256)S(1)}, u32[]{:S(2)}) copy-start(f32[256]{0:T(256)S(1)} %convert_element_type.183) | copy-start | bytes 3076
  105.0 64.9 %copy-start.6 = (f32[1176,256]{1,0:T(8,128)}, f32[1176,256]{1,0:T(8,128)S(1)}, u32[]{:S(2)}) copy-start(f32[1176,256]{1,0:T(8,128)S(1)} %get-tuple-element.211) | copy-start | bytes 3612676
  174.7 99.7 %copy-start.105 = (f32[256]{0:T(256)}, f32[256]{0:T(256)S(1)}, u32[]{:S(2)}) copy-start(f32[256]{0:T(256)S(1)} %convert_element_type.185) | copy-start | bytes 3076
  174.8 99.7 %copy-start.107 = (f32[256]{0:T(256)}, f32[256]{0:T(256)S(1)}, u32[]{:S(2)}) copy-start(f32[256]{0:T(256)S(1)} %convert_element_type.186) | copy-start | bytes 3076
  221.6 98.4 %copy-start.61 = (f32[1024]{0:T(1024)}, f32[1024]{0:T(1024)S(1)}, u32[]{:S(2)}) copy-start(f32[1024]{0:T(1024)S(1)} %convert_element_type.188) | copy-start | bytes 12292
  221.6 98.4 %copy-start.63 = (f32[1024]{0:T(1024)}, f32[1024]{0:T(1024)S(1)}, u32[]{:S(2)}) copy-start(f32[1024]{0:T(1024)S(1)} %convert_element_type.189) | copy-start | bytes 12292
  223.0 128.9 %copy-start.41 = (f32[768]{0:T(1024)}, f32[768]{0:T(1024)S(1)}, u32[]{:S(2)}) copy-start(f32[768]{0:T(1024)S(1)} %convert_element_type.195) | copy-start | bytes 9220
  509.1 101.0 %copy-start.33 = (f32[1560]{0:T(1024)}, f32[1560]{0:T(1024)S(1)}, u32[]{:S(2)}) copy-start(f32[1560]{0:T(1024)S(1)} %broadcast_multiply_fusion.1) | copy-start | bytes 18724
  511.9 98.3 %copy-start.47 = (f32[1560]{0:T(1024)}, f32[1560]{0:T(1024)S(1)}, u32[]{:S(2)}) copy-start(f32[1560]{0:T(1024)S(1)} %fusion.61) | copy-start | bytes 18724
  849.8 268.6 %reduce-scatter.25.cloned.1.call-start = ((), (), s32[]{:S(2)}) async-start(), calls=%async_computation.21 | async-start | bytes 1081344
  978.2 241.2 %reduce-scatter.19.cloned.1.call-start = ((), (), s32[]{:S(2)}) async-start(), calls=%async_computation.18 | async-start | bytes 2433024 | tf_op jit(solution)/shard_map/reduce_scatter | solution.py:424
  983.7 340.3 %reduce-scatter.11.cloned.1.call-start = ((), (), s32[]{:S(2)}) async-start(), calls=%async_computation.14 | async-start | bytes 2433024 | tf_op jit(solution)/shard_map/reduce_scatter | solution.py:416
  990.0 440.7 %reduce-scatter.15.cloned.1.call-start = ((), (), s32[]{:S(2)}) async-start(), calls=%async_computation.16 | async-start | bytes 3244032 | tf_op jit(solution)/shard_map/reduce_scatter | solution.py:418
  995.5 559.4 %reduce-scatter.17.cloned.1.call-start = ((), (), s32[]{:S(2)}) async-start(), calls=%async_computation.17 | async-start | bytes 7299072 | tf_op jit(solution)/shard_map/reduce_scatter | solution.py:422
  1011.6 685.7 %reduce-scatter.23.cloned.1.call-start = ((), (), s32[]{:S(2)}) async-start(), calls=%async_computation.20 | async-start | bytes 9732096 | tf_op jit(solution)/shard_map/reduce_scatter | solution.py:430
  1032.4 805.6 %reduce-scatter.21.cloned.1.call-start = ((), (), s32[]{:S(2)}) async-start(), calls=%async_computation.19 | async-start | bytes 9732096 | tf_op jit(solution)/shard_map/reduce_scatter | solution.py:428
  (95 other events, 1465.0 us)
Sparse Core Ops, SparseCore 0:
  11.2 57.3 all-gather.6
  71.7 54.3 all-gather.8
  129.1 59.8 all-gather.10
  191.9 52.4 all-gather.12
  247.2 63.2 all-gather.14
  313.4 62.1 all-gather.16
  849.9 134.0 reduce-scatter.12
  986.9 131.3 reduce-scatter.24
  1124.2 95.2 reduce-scatter.18
  1226.0 97.9 reduce-scatter.10
  1330.1 100.5 reduce-scatter.14
  1436.8 118.1 reduce-scatter.16
  1562.4 134.7 reduce-scatter.22
  1703.6 134.3 reduce-scatter.20
where the time goes:
time: 1860 us; the launch traced here: 1840 us
  waiting for transfers between devices  770 us (41%)
  blocking collectives  373 us (20%)
  matrix products  307 us (17%)
  local copies, waits for them, and re-layouts  249 us (13%)
  other arithmetic  129 us (7%)
    reduce_scatter x1, waiting for transfers between devices, local(): lax.psum_scatter(g_down, ('dp', 'fsdp'), scatter_dimension=0, tiled=True)  142 us
    reduce_scatter x1, waiting for transfers between devices, local(): lax.psum_scatter(g_up, ('dp', 'fsdp'), scatter_dimension=0, tiled=True)  141 us
    reduce_scatter x1, waiting for transfers between devices, local(): lax.psum_scatter(g_qkv, ('dp', 'fsdp'), scatter_dimension=0, tiled=True)  124 us
    psum x3, blocking collectives, batch_backward(): lax.psum((jnp.sum(grad_shift, 0), jnp.sum(grad_shift * norm_part, 0)), ('...  123 us
    psum x3, blocking collectives, batch_forward(): lax.psum((jnp.sum(pre_values, 0), jnp.sum(pre_values * pre_values, 0)), (...  120 us
    reduce_scatter x1, waiting for transfers between devices, local(): lax.psum_scatter(g_patch, ('dp', 'fsdp'), scatter_dimension=0, tiled=True)  107 us
    reduce_scatter x1, waiting for transfers between devices, local(): lax.psum_scatter(g_conv, ('dp', 'fsdp'), scatter_dimension=0, tiled=True)  105 us
    reduce_scatter x1, waiting for transfers between devices, local(): lax.psum_scatter(g_out, ('dp', 'fsdp'), scatter_dimension=0, tiled=True)  101 us
  transfers between devices with their start and end apart: 14, of which 7 were waited for; matrix products, arithmetic and copies ran while one was open for 21% of the time, Pallas kernels for 0%

commit v1 on v0

--- a/solution.py
+++ b/solution.py
@@ -1,6 +1,10 @@
+import functools
+
 import jax
 import jax.numpy as jnp
 from jax import lax
+from jax.experimental import pallas as pl
+from jax.experimental.pallas import tpu as pltpu
 from jax.sharding import PartitionSpec as P
 
 HEAD_DIM = 64
@@ -10,6 +14,332 @@
 ln_eps = 1e-06
 bn_eps = 1e-05
 gelu_coef = 0.7978845608028654
+
+
+MESH = pl.DeviceIdType.MESH
+DMA = pltpu.SemaphoreType.DMA
+
+
+def rcopy(src, dst, send, recv, dev):
+    return pltpu.make_async_remote_copy(
+        src_ref=src, dst_ref=dst, send_sem=send, recv_sem=recv, device_id=dev, device_id_type=MESH
+    )
+
+
+class Place:
+    def __init__(self, A, B):
+        self.A, self.B, self.A2, self.Z = A, B, A // 2, B // 2
+        a, b = lax.axis_index("dp"), lax.axis_index("fsdp")
+        self.a, self.b = a, b
+        self.y, self.x = a // 2, lax.rem(a, 2)
+        self.z, self.c = b // 2, lax.rem(b, 2)
+        self.zs = [lax.rem(self.z + k, self.Z) for k in range(1, self.Z)]
+        self.ys = [lax.rem(self.y + k, self.A2) for k in range(1, self.A2)]
+        self.zfrom = [lax.rem(self.z + self.Z - k, self.Z) for k in range(1, self.Z)]
+        self.yfrom = [lax.rem(self.y + self.A2 - k, self.A2) for k in range(1, self.A2)]
+        self.me = (a, b)
+        self.core = (a, self.z * 2 + 1 - self.c)
+        self.xpeer = (self.y * 2 + 1 - self.x, b)
+        self.zpeers = [(a, zz * 2 + self.c) for zz in self.zs]
+        self.ypeers = [(yy * 2 + self.x, b) for yy in self.ys]
+
+    def greet(self):
+        peers = self.zpeers + self.ypeers + [self.xpeer, self.core]
+        bar = pltpu.get_barrier_semaphore()
+        for p in peers:
+            pl.semaphore_signal(bar, inc=1, device_id=p, device_id_type=MESH)
+        pl.semaphore_wait(bar, len(peers))
+
+
+class GatherItem:
+    def __init__(self, pc, i, cols, order, src, out, sems):
+        self.pc, self.order, self.src = pc, order, src
+        self.o = out if cols is None else out.at[:, :, :, :, :, pl.ds(*cols)]
+        if cols is not None:
+            self.src = src.at[:, pl.ds(*cols)]
+        self.loc, self.s1, self.r1, self.s2, self.r2, self.s3, self.r3, self.sc, self.rc = [s.at[i] for s in sems]
+        self.sends, self.corew = [], []
+
+    def go(self, d):
+        d.start()
+        self.sends.append(d)
+
+    def core(self, j, got, mirror):
+        self.go(rcopy(got, got, self.sc.at[j], self.rc.at[j], self.pc.core))
+        self.corew.append((j, mirror))
+
+    def start(self):
+        p = self.pc
+        mine = self.o.at[p.y, p.x, p.z, p.c]
+        self.local = pltpu.make_async_copy(self.src, mine, self.loc)
+        self.local.start()
+        for k, dev in enumerate(p.zpeers):
+            self.go(rcopy(self.src, mine, self.s1.at[k], self.r1.at[k], dev))
+
+    def second(self):
+        p = self.pc
+        self.local.wait()
+        for k, zz in enumerate(p.zfrom):
+            got = self.o.at[p.y, p.x, zz, p.c]
+            rcopy(got, got, self.s1.at[k], self.r1.at[k], p.me).wait_recv()
+        col = self.o.at[p.y, p.x, :, p.c]
+        for k, dev in enumerate([p.xpeer] if self.order == 0 else p.ypeers):
+            self.go(rcopy(col, col, self.s2.at[k], self.r2.at[k], dev))
+        self.core(0, col, self.o.at[p.y, p.x, :, 1 - p.c])
+
+    def third(self):
+        p, o = self.pc, self.o
+        froms = [(p.y, 1 - p.x)] if self.order == 0 else [(yy, p.x) for yy in p.yfrom]
+        blk = o.at[p.y, :, :, p.c] if self.order == 0 else o.at[:, p.x, :, p.c]
+        for k, (yy, xx) in enumerate(froms):
+            got = o.at[yy, xx, :, p.c]
+            rcopy(got, got, self.s2.at[k], self.r2.at[k], p.me).wait_recv()
+        for k, dev in enumerate(p.ypeers if self.order == 0 else [p.xpeer]):
+            self.go(rcopy(blk, blk, self.s3.at[k], self.r3.at[k], dev))
+        for k, (yy, xx) in enumerate(froms):
+            self.core(1 + k, o.at[yy, xx, :, p.c], o.at[yy, xx, :, 1 - p.c])
+
+    def fourth(self):
+        p, o = self.pc, self.o
+        base = 1 + (1 if self.order == 0 else p.A2 - 1)
+        froms = [((yy, slice(None)),) for yy in p.yfrom] if self.order == 0 else [None]
+        if self.order == 0:
+            gots = [(o.at[yy, :, :, p.c], o.at[yy, :, :, 1 - p.c]) for yy in p.yfrom]
+        else:
+            gots = [(o.at[:, 1 - p.x, :, p.c], o.at[:, 1 - p.x, :, 1 - p.c])]
+        for k, (got, mirror) in enumerate(gots):
+            rcopy(got, got, self.s3.at[k], self.r3.at[k], p.me).wait_recv()
+            self.core(base + k, got, mirror)
+
+    def arrived(self):
+        for j, got in self.corew:
+            rcopy(got, got, self.sc.at[j], self.rc.at[j], self.pc.me).wait_recv()
+
+    def drain(self):
+        for d in self.sends:
+            d.wait_send()
+
+
+def gather_sems(A, B, n):
+    A2, Z = A // 2, B // 2
+    m = max(A2 - 1, 1)
+    return [DMA((n,)), DMA((n, Z - 1)), DMA((n, Z - 1)), DMA((n, m)), DMA((n, m)), DMA((n, m)), DMA((n, m)), DMA((n, A2 + 1)), DMA((n, A2 + 1))]
+
+
+def wave(items, lags, stages):
+    last = len(items) + lags[-1]
+    for t in range(last):
+        for lag, stage in zip(reversed(lags), reversed(stages)):
+            if 0 <= t - lag < len(items):
+                getattr(items[t - lag], stage)()
+
+
+def gather_kernel(A, B, items, n, lags, *refs):
+    ins, outs, sems = refs[:n], refs[n : 2 * n], refs[2 * n :]
+    pc = Place(A, B)
+    pc.greet()
+    moves = [GatherItem(pc, j, cols, order, ins[i], outs[i], sems) for j, (i, cols, order) in enumerate(items)]
+    wave(moves, lags, ["start", "second", "third", "fourth"])
+    for m in moves:
+        m.arrived()
+    for m in moves:
+        m.drain()
+
+
+def cut(widths_parts):
+    items, order = [], 0
+    for i, (width, parts) in enumerate(widths_parts):
+        for q in range(parts):
+            items.append((i, None if parts == 1 else (q * (width // parts), width // parts), order))
+            order = 1 - order
+    return items
+
+
+def gather(A, B, shards, parts, cid, lags=(0, 2, 4, 6)):
+    n = len(shards)
+    A2, Z = A // 2, B // 2
+    items = cut([(s.shape[1], q) for s, q in zip(shards, parts)])
+    return pl.pallas_call(
+        functools.partial(gather_kernel, A, B, items, n, lags),
+        out_shape=[jax.ShapeDtypeStruct((A2, 2, Z, 2) + s.shape, s.dtype) for s in shards],
+        in_specs=[pl.BlockSpec(memory_space=pl.ANY)] * n,
+        out_specs=[pl.BlockSpec(memory_space=pl.ANY)] * n,
+        scratch_shapes=gather_sems(A, B, len(items)),
+        compiler_params=pltpu.CompilerParams(collective_id=cid, has_side_effects=True),
+        name="gather",
+    )(*shards)
+
+
+class ScatterItem:
+    def __init__(self, pc, i, order, src, out, own, r0, r1, r2, r3, sems):
+        self.pc, self.order, self.src, self.out = pc, order, src, out
+        self.own, self.r0, self.r1, self.r2, self.r3 = own, r0, r1, r2, r3
+        self.loc, self.s0, self.q0, self.s1, self.q1, self.s2, self.q2, self.s3, self.q3 = [s.at[i] for s in sems]
+        self.sends = []
+
+    def go(self, d):
+        d.start()
+        self.sends.append(d)
+
+    def start(self):
+        p = self.pc
+        self.go(rcopy(self.src.at[:, :, :, 1 - p.c], self.r0, self.s0, self.q0, p.core))
+        self.local = pltpu.make_async_copy(self.src.at[:, :, :, p.c], self.own, self.loc)
+        self.local.start()
+
+    def add(self, dst, others, lead):
+        total = 1
+        for d in lead:
+            total *= d
+
+        def body(t, _):
+            idx, rest = [], t
+            for d in reversed(lead):
+                idx.append(lax.rem(rest, d))
+                rest = rest // d
+            idx = tuple(reversed(idx))
+            v = dst[idx].astype(jnp.float32)
+            for o in others:
+                v = v + o[idx].astype(jnp.float32)
+            dst[idx] = v.astype(jnp.bfloat16)
+            return 0
+
+        lax.fori_loop(0, total, body, 0)
+
+    def second(self):
+        p = self.pc
+        self.local.wait()
+        rcopy(self.r0, self.r0, self.s0, self.q0, p.me).wait_recv()
+        self.add(self.own, [self.r0], (p.A2, 2, p.Z))
+        if self.order == 0:
+            self.go(rcopy(self.own.at[:, 1 - p.x], self.r1.at[0], self.s1.at[0], self.q1.at[0], p.xpeer))
+        else:
+            for k, yy in enumerate(p.ys):
+                self.go(rcopy(self.own.at[yy], self.r1.at[k], self.s1.at[k], self.q1.at[k], p.ypeers[k]))
+
+    def third(self):
+        p = self.pc
+        n1 = 1 if self.order == 0 else p.A2 - 1
+        for k in range(n1):
+            rcopy(self.r1.at[k], self.r1.at[k], self.s1.at[k], self.q1.at[k], p.me).wait_recv()
+        mine = self.own.at[:, p.x] if self.order == 0 else self.own.at[p.y]
+        self.add(mine, [self.r1.at[k] for k in range(n1)], (p.A2 if self.order == 0 else 2, p.Z))
+        if self.order == 0:
+            for k, yy in enumerate(p.ys):
+                self.go(rcopy(self.own.at[yy, p.x], self.r2.at[k], self.s2.at[k], self.q2.at[k], p.ypeers[k]))
+        else:
+            self.go(rcopy(self.own.at[p.y, 1 - p.x], self.r2.at[0], self.s2.at[0], self.q2.at[0], p.xpeer))
+
+    def fourth(self):
+        p = self.pc
+        n2 = p.A2 - 1 if self.order == 0 else 1
+        for k in range(n2):
+            rcopy(self.r2.at[k], self.r2.at[k], self.s2.at[k], self.q2.at[k], p.me).wait_recv()
+        self.add(self.own.at[p.y, p.x], [self.r2.at[k] for k in range(n2)], (p.Z,))
+        for k, zz in enumerate(p.zs):
+            self.go(rcopy(self.own.at[p.y, p.x, zz], self.r3.at[k], self.s3.at[k], self.q3.at[k], p.zpeers[k]))
+
+    def arrived(self):
+        p = self.pc
+        for k in range(p.Z - 1):
+            rcopy(self.r3.at[k], self.r3.at[k], self.s3.at[k], self.q3.at[k], p.me).wait_recv()
+        v = self.own[p.y, p.x, p.z].astype(jnp.float32)
+        for k in range(p.Z - 1):
+            v = v + self.r3[k].astype(jnp.float32)
+        self.out[...] = v
+
+    def drain(self):
+        for d in self.sends:
+            d.wait_send()
+
+
+def scatter_sems(A, B, n):
+    m, Z = max(A // 2 - 1, 1), B // 2
+    return [DMA((n,)), DMA((n,)), DMA((n,)), DMA((n, m)), DMA((n, m)), DMA((n, m)), DMA((n, m)), DMA((n, Z - 1)), DMA((n, Z - 1))]
+
+
+def scatter_scratch(A, B, shape, order):
+    A2, Z = A // 2, B // 2
+    n1 = (1, A2, Z) if order == 0 else (A2 - 1, 2, Z)
+    n2 = (A2 - 1, Z) if order == 0 else (1, Z)
+    return [pltpu.VMEM(s + shape, jnp.bfloat16) for s in ((A2, 2, Z), (A2, 2, Z), n1, n2, (Z - 1,))]
+
+
+def scatter_kernel(A, B, orders, lags, n, *refs):
+    ins, outs, bufs, sems = refs[:n], refs[n : 2 * n], refs[2 * n : 7 * n], refs[7 * n :]
+    pc = Place(A, B)
+    pc.greet()
+    moves = [ScatterItem(pc, i, orders[i], ins[i], outs[i], *bufs[5 * i : 5 * i + 5], sems) for i in range(n)]
+    wave(moves, lags, ["start", "second", "third", "fourth", "arrived"])
+    for m in moves:
+        m.drain()
+
+
+def scatter(A, B, grads, cid, lags=(0, 1, 3, 5, 7)):
+    n = len(grads)
+    A2, Z = A // 2, B // 2
+    shapes = [(g.shape[0] // (A * B), g.shape[1]) for g in grads]
+    orders = [i % 2 for i in range(n)]
+    scratch = []
+    for s, o in zip(shapes, orders):
+        scratch += scatter_scratch(A, B, s, o)
+    return pl.pallas_call(
+        functools.partial(scatter_kernel, A, B, orders, lags, n),
+        out_shape=[jax.ShapeDtypeStruct(s, jnp.float32) for s in shapes],
+        in_specs=[pl.BlockSpec(memory_space=pl.ANY)] * n,
+        out_specs=[pl.BlockSpec(memory_space=pltpu.VMEM)] * n,
+        scratch_shapes=scratch + scatter_sems(A, B, n),
+        compiler_params=pltpu.CompilerParams(collective_id=cid, has_side_effects=True, vmem_limit_bytes=56 << 20),
+        name="scatter",
+    )(*[g.reshape((A2, 2, Z, 2) + s) for g, s in zip(grads, shapes)])
+
+
+def flips(A, B):
+    a, b = lax.axis_index("dp"), lax.axis_index("fsdp")
+    out = []
+    bit = 1
+    while bit < B:
+        out.append((a, b + bit - 2 * bit * lax.rem(b // bit, 2)))
+        bit *= 2
+    bit = 1
+    while bit < A:
+        out.append((a + bit - 2 * bit * lax.rem(a // bit, 2), b))
+        bit *= 2
+    return out
+
+
+def total_kernel(A, B, x_ref, o_ref, out_buf, in_buf, ssem, rsem):
+    peers = flips(A, B)
+    bar = pltpu.get_barrier_semaphore()
+    for p in peers:
+        pl.semaphore_signal(bar, inc=1, device_id=p, device_id_type=MESH)
+    pl.semaphore_wait(bar, len(peers))
+    v = x_ref[...]
+    sends = []
+    for k, p in enumerate(peers):
+        out_buf[k] = v
+        d = rcopy(out_buf.at[k], in_buf.at[k], ssem.at[k], rsem.at[k], p)
+        d.start()
+        sends.append(d)
+        d.wait_recv()
+        v = v + in_buf[k]
+    o_ref[...] = v
+    for d in sends:
+        d.wait_send()
+
+
+def total(A, B, x, cid):
+    h = (A.bit_length() - 1) + (B.bit_length() - 1)
+    vm = pl.BlockSpec(memory_space=pltpu.VMEM)
+    return pl.pallas_call(
+        functools.partial(total_kernel, A, B),
+        out_shape=jax.ShapeDtypeStruct(x.shape, x.dtype),
+        in_specs=[vm],
+        out_specs=vm,
+        scratch_shapes=[pltpu.VMEM((h,) + x.shape, x.dtype), pltpu.VMEM((h,) + x.shape, x.dtype), DMA((h,)), DMA((h,))],
+        compiler_params=pltpu.CompilerParams(collective_id=cid, has_side_effects=True),
+        name="total",
+    )(x)
 
 
 def smooth(values):
@@ -53,10 +383,38 @@
     )
 
 
+def summed(first, second):
+    A, B = lax.axis_size("dp"), lax.axis_size("fsdp")
+    width = first.shape[0]
+    if width < 1024:
+        first, second = (jnp.pad(v, (0, 1024 - width)) for v in (first, second))
+    both = total(A, B, jnp.pad(jnp.stack([first, second]), ((0, 6), (0, 0))), 2)
+    return both[0, :width], both[1, :width]
+
+
+def vectors_summed(vectors):
+    A, B = lax.axis_size("dp"), lax.axis_size("fsdp")
+    flat = jnp.concatenate(vectors)
+    wide = total(A, B, flat.reshape(-1, 128), 3).reshape(-1)
+    out, at = [], 0
+    for v in vectors:
+        out.append(wide[at : at + v.shape[0]])
+        at += v.shape[0]
+    return out
+
+
+def gather_all(matrices, vectors):
+    A, B = lax.axis_size("dp"), lax.axis_size("fsdp")
+    pack = jnp.pad(jnp.stack([jnp.pad(v, (0, 128 - v.shape[0])) for v in vectors]), ((0, 32 - len(vectors)), (0, 0)))
+    parts = (1, 1, 1, 1, 1, 3, 1, 4, 3)
+    got = gather(A, B, [pack] + list(matrices), parts, 0)
+    whole = [g.reshape((-1,) + g.shape[-1:]) for g in got[1:]]
+    table = got[0].reshape(-1, 32, 128)
+    return whole, [table[:, i, : v.shape[0]].reshape(-1) for i, v in enumerate(vectors)]
+
+
 def batch_forward(pre_values, gain_vec, shift_vec):
-    column_sum, column_squares = lax.psum(
-        (jnp.sum(pre_values, 0), jnp.sum(pre_values * pre_values, 0)), ("dp", "fsdp")
-    )
+    column_sum, column_squares = summed(jnp.sum(pre_values, 0), jnp.sum(pre_values * pre_values, 0))
     total_rows = pre_values.shape[0] * lax.axis_size(("dp", "fsdp"))
     batch_mean = column_sum / total_rows
     inv_std = lax.rsqrt(column_squares / total_rows - batch_mean * batch_mean + bn_eps)
@@ -70,9 +428,7 @@
 
 def batch_backward(grad_shift, norm_part, inv_std, gain_vec):
     total_rows = grad_shift.shape[0] * lax.axis_size(("dp", "fsdp"))
-    total_bias, total_gain = lax.psum(
-        (jnp.sum(grad_shift, 0), jnp.sum(grad_shift * norm_part, 0)), ("dp", "fsdp")
-    )
+    total_bias, total_gain = summed(jnp.sum(grad_shift, 0), jnp.sum(grad_shift * norm_part, 0))
     grad_pre = (
         inv_std
         * gain_vec.astype(jnp.float32)
@@ -238,57 +594,10 @@
     w_down,
     b_down,
 ):
-    gathered = (
-        lax.all_gather(w_red, ("dp", "fsdp"), axis=0, tiled=True),
-        lax.all_gather(bn1_gain, ("dp", "fsdp"), axis=0, tiled=True),
-        lax.all_gather(bn1_bias, ("dp", "fsdp"), axis=0, tiled=True),
-        lax.all_gather(w_conv, ("dp", "fsdp"), axis=0, tiled=True),
-        lax.all_gather(bn2_gain, ("dp", "fsdp"), axis=0, tiled=True),
-        lax.all_gather(bn2_bias, ("dp", "fsdp"), axis=0, tiled=True),
-        lax.all_gather(w_exp, ("dp", "fsdp"), axis=0, tiled=True),
-        lax.all_gather(bn3_gain, ("dp", "fsdp"), axis=0, tiled=True),
-        lax.all_gather(bn3_bias, ("dp", "fsdp"), axis=0, tiled=True),
-        lax.all_gather(w_patch, ("dp", "fsdp"), axis=0, tiled=True),
-        lax.all_gather(b_patch, ("dp", "fsdp"), axis=0, tiled=True),
-        lax.all_gather(ln1_gain, ("dp", "fsdp"), axis=0, tiled=True),
-        lax.all_gather(ln1_bias, ("dp", "fsdp"), axis=0, tiled=True),
-        lax.all_gather(w_qkv, ("dp", "fsdp"), axis=0, tiled=True),
-        lax.all_gather(b_qv, ("dp", "fsdp"), axis=0, tiled=True),
-        lax.all_gather(w_out, ("dp", "fsdp"), axis=0, tiled=True),
-        lax.all_gather(b_out, ("dp", "fsdp"), axis=0, tiled=True),
-        lax.all_gather(ln2_gain, ("dp", "fsdp"), axis=0, tiled=True),
-        lax.all_gather(ln2_bias, ("dp", "fsdp"), axis=0, tiled=True),
-        lax.all_gather(w_up, ("dp", "fsdp"), axis=0, tiled=True),
-        lax.all_gather(b_up, ("dp", "fsdp"), axis=0, tiled=True),
-        lax.all_gather(w_down, ("dp", "fsdp"), axis=0, tiled=True),
-        lax.all_gather(b_down, ("dp", "fsdp"), axis=0, tiled=True),
-    )
+    mats, vecs = gather_all((w_red, w_conv, w_exp, w_patch, w_qkv, w_out, w_up, w_down), (bn1_gain, bn1_bias, bn2_gain, bn2_bias, bn3_gain, bn3_bias, b_patch, ln1_gain, ln1_bias, b_qv, b_out, ln2_gain, ln2_bias, b_up, b_down))
+    gathered = (mats[0], vecs[0], vecs[1], mats[1], vecs[2], vecs[3], mats[2], vecs[4], vecs[5], mats[3], vecs[6], vecs[7], vecs[8], mats[4], vecs[9], mats[5], vecs[10], vecs[11], vecs[12], mats[6], vecs[13], mats[7], vecs[14])
     output, saved = forward_pass(feats, text, lengths, gathered)
-    weights = (
-        lax.all_gather(w_red, ("dp", "fsdp"), axis=0, tiled=True),
-        lax.all_gather(bn1_gain, ("dp", "fsdp"), axis=0, tiled=True),
-        lax.all_gather(bn1_bias, ("dp", "fsdp"), axis=0, tiled=True),
-        lax.all_gather(w_conv, ("dp", "fsdp"), axis=0, tiled=True),
-        lax.all_gather(bn2_gain, ("dp", "fsdp"), axis=0, tiled=True),
-        lax.all_gather(bn2_bias, ("dp", "fsdp"), axis=0, tiled=True),
-        lax.all_gather(w_exp, ("dp", "fsdp"), axis=0, tiled=True),
-        lax.all_gather(bn3_gain, ("dp", "fsdp"), axis=0, tiled=True),
-        lax.all_gather(bn3_bias, ("dp", "fsdp"), axis=0, tiled=True),
-        lax.all_gather(w_patch, ("dp", "fsdp"), axis=0, tiled=True),
-        lax.all_gather(b_patch, ("dp", "fsdp"), axis=0, tiled=True),
-        lax.all_gather(ln1_gain, ("dp", "fsdp"), axis=0, tiled=True),
-        lax.all_gather(ln1_bias, ("dp", "fsdp"), axis=0, tiled=True),
-        lax.all_gather(w_qkv, ("dp", "fsdp"), axis=0, tiled=True),
-        lax.all_gather(b_qv, ("dp", "fsdp"), axis=0, tiled=True),
-        lax.all_gather(w_out, ("dp", "fsdp"), axis=0, tiled=True),
-        lax.all_gather(b_out, ("dp", "fsdp"), axis=0, tiled=True),
-        lax.all_gather(ln2_gain, ("dp", "fsdp"), axis=0, tiled=True),
-        lax.all_gather(ln2_bias, ("dp", "fsdp"), axis=0, tiled=True),
-        lax.all_gather(w_up, ("dp", "fsdp"), axis=0, tiled=True),
-        lax.all_gather(b_up, ("dp", "fsdp"), axis=0, tiled=True),
-        lax.all_gather(w_down, ("dp", "fsdp"), axis=0, tiled=True),
-        lax.all_gather(b_down, ("dp", "fsdp"), axis=0, tiled=True),
-    )
+    weights = gathered
     (
         full_red,
         full_bn1_gain,
@@ -411,41 +720,11 @@
         .astype(jnp.bfloat16)
         .reshape(examples, patches, channels)
     )
-    shares = (
-        lax.psum_scatter(g_red, ("dp", "fsdp"), scatter_dimension=0, tiled=True),
-        lax.psum_scatter(g_conv, ("dp", "fsdp"), scatter_dimension=0, tiled=True),
-        lax.psum_scatter(g_exp, ("dp", "fsdp"), scatter_dimension=0, tiled=True),
-        lax.psum_scatter(g_patch, ("dp", "fsdp"), scatter_dimension=0, tiled=True),
-        lax.psum_scatter(g_b_patch, ("dp", "fsdp"), scatter_dimension=0, tiled=True),
-        lax.psum_scatter(g_ln1_gain, ("dp", "fsdp"), scatter_dimension=0, tiled=True),
-        lax.psum_scatter(g_ln1_bias, ("dp", "fsdp"), scatter_dimension=0, tiled=True),
-        lax.psum_scatter(g_qkv, ("dp", "fsdp"), scatter_dimension=0, tiled=True),
-        lax.psum_scatter(g_b_qv, ("dp", "fsdp"), scatter_dimension=0, tiled=True),
-        lax.psum_scatter(g_out, ("dp", "fsdp"), scatter_dimension=0, tiled=True),
-        lax.psum_scatter(g_b_out, ("dp", "fsdp"), scatter_dimension=0, tiled=True),
-        lax.psum_scatter(g_ln2_gain, ("dp", "fsdp"), scatter_dimension=0, tiled=True),
-        lax.psum_scatter(g_ln2_bias, ("dp", "fsdp"), scatter_dimension=0, tiled=True),
-        lax.psum_scatter(g_up, ("dp", "fsdp"), scatter_dimension=0, tiled=True),
-        lax.psum_scatter(g_b_up, ("dp", "fsdp"), scatter_dimension=0, tiled=True),
-        lax.psum_scatter(g_down, ("dp", "fsdp"), scatter_dimension=0, tiled=True),
-        lax.psum_scatter(g_b_down, ("dp", "fsdp"), scatter_dimension=0, tiled=True),
-    )
-    s_red, s_conv, s_exp, s_patch, s_b_patch = shares[:5]
-    block_shares = shares[5:]
-    (
-        s_ln1_gain,
-        s_ln1_bias,
-        s_qkv,
-        s_b_qv,
-        s_out,
-        s_b_out,
-        s_ln2_gain,
-        s_ln2_bias,
-        s_up,
-        s_b_up,
-        s_down,
-        s_b_down,
-    ) = block_shares
+    A, B = lax.axis_size("dp"), lax.axis_size("fsdp")
+    (s_red, s_conv, s_exp, s_patch, s_qkv, s_out, s_up, s_down) = scatter(A, B, [w.astype(jnp.bfloat16) for w in (g_red, g_conv, g_exp, g_patch, g_qkv, g_out, g_up, g_down)], 1)
+    small = (g_b_patch, g_ln1_gain, g_ln1_bias, g_b_qv, g_b_out, g_ln2_gain, g_ln2_bias, g_b_up, g_b_down)
+    sizes = (b_patch.shape[0], ln1_gain.shape[0], ln1_bias.shape[0], b_qv.shape[0], b_out.shape[0], ln2_gain.shape[0], ln2_bias.shape[0], b_up.shape[0], b_down.shape[0])
+    (s_b_patch, s_ln1_gain, s_ln1_bias, s_b_qv, s_b_out, s_ln2_gain, s_ln2_bias, s_b_up, s_b_down) = [own_share(w, n) for w, n in zip(vectors_summed(small), sizes)]
     narrow = bn1_gain.shape[0]
     broad = bn3_gain.shape[0]
     return (

time: 1860 us -> 1000 us (0.54)
  waiting for transfers between devices: 770 us -> 0 us
  blocking collectives: 373 us -> 0 us
  Pallas kernels: 0 us -> 319 us
  matrix products: 307 us -> 286 us
    reduce_scatter x7 -> x0, waiting for transfers between devices: 720 us -> none  [the longest x1 142 us: local(): lax.psum_scatter(g_down, ('dp', 'fsdp'), scatter_dimension=0, tiled=True)]
    pallas_call x0 -> x9, Pallas kernels: none -> 319 us  [the longest x1 115 us: scatter(): pl.pallas_call(functools.partial(scatter_kernel, A, B, orders, lags, n),...]
    psum x6 -> x0, blocking collectives: 243 us -> none  [the longest x3 123 us: batch_backward(): lax.psum((jnp.sum(grad_shift, 0), jnp.sum(grad_shift * norm_part, 0)), ('...]
    all_gather x2 -> x0, blocking collectives: 92.5 us -> none  [the longest x1 46.8 us: local(): lax.all_gather(w_exp, ('dp', 'fsdp'), axis=0, tiled=True)]
    unnamed x15 -> x0, waiting for transfers between devices: 50.7 us -> none
    unnamed x1 -> x0, blocking collectives: 37.6 us -> none
    unnamed x277 -> x249, local copies, waits for them, and re-layouts: 69.3 us -> 44.2 us
    another operation x0 -> x10, local copies, waits for them, and re-layouts: none -> 19.1 us  [the longest x1 13.6 us: local(): jnp.stack([g_query, g_key, g_value], 2).astype(jnp.bfloat16)]
  transfers between devices with their start and end apart: 14 -> 0, of which waited for: 7 -> 0; matrix products, arithmetic and copies ran while one was open for 21% -> 0% of each run, Pallas kernels for 0% -> 0%
where the time goes in v1:
time: 1000 us; the launch traced here: 985 us
  Pallas kernels  319 us (32%)
  matrix products  286 us (29%)
  local copies, waits for them, and re-layouts  242 us (24%)
  other arithmetic  135 us (14%)
    pallas_call x1, Pallas kernels, scatter(): pl.pallas_call(functools.partial(scatter_kernel, A, B, orders, lags, n),...  115 us
    pallas_call x7, Pallas kernels, total(): pl.pallas_call(functools.partial(total_kernel, A, B), out_shape=jax.Shape...  111 us
    pallas_call x1, Pallas kernels, gather(): pl.pallas_call(functools.partial(gather_kernel, A, B, items, n, lags), ou...  92.9 us
    dot_general x8, matrix products, right_product(): lax.dot_general(left, right, (((1,), (1,)), ((), ())), preferred_element_...  80.4 us
    dot_general x8, matrix products, left_product(): lax.dot_general(left, right, (((0,), (0,)), ((), ())), preferred_element_...  62.9 us
    dot_general x8, matrix products, matmul(): return jnp.dot(left, right, preferred_element_type=jnp.float32)  59.3 us
    unnamed x249, local copies, waits for them, and re-layouts  44.2 us
    sub x1, other arithmetic, forward_pass(): expo_scores = jnp.exp(scores - top_score)  37.4 us

profile of v1, /device:TPU:0, one launch (start us, length us, event | category | flops | bytes accessed | tf_op | source)
XLA Modules:
  0.0 985.3 jit_solution(13421612988967448586)
XLA Ops:
  13.6 92.9 %gather.1 = (bf16[2,2,4,2,32,128]{5,4,3,2,1,0:T(8,128)(2,1)}, bf16[2,2,4,2,32,256]{5,4,3,2,1,0:T(8,128)(2,1)}, bf16[2,2,4,2,72,256]{5,4,3,2,1,0:T(8,128)(2,1)}, ...) custom-call(bf16[32,128]{1,0:T(8,128)(2,1)} %pad.150.refs_0_, ...), custom_call_target="tpu_custom_call" | custom-call | tf_op jit(solution)/shard_map/gather/pallas_call | solution.py:162
  120.6 18.2 %total.7 = f32[8,1024]{1,0:T(8,128)} custom-call(f32[8,1024]{1,0:T(8,128)} %select_maximum_fusion.5.x_ref), custom_call_target="tpu_custom_call" | custom-call | tf_op jit(solution)/shard_map/total/pallas_call | solution.py:334
  171.6 14.4 %total.8 = f32[8,1024]{1,0:T(8,128)} custom-call(f32[8,1024]{1,0:T(8,128)} %select_maximum_fusion.4.x_ref), custom_call_target="tpu_custom_call" | custom-call | tf_op jit(solution)/shard_map/total/pallas_call | solution.py:334
  191.5 16.5 %total.9 = f32[8,1024]{1,0:T(8,128)} custom-call(f32[8,1024]{1,0:T(8,128)} %select_maximum_fusion.3.x_ref), custom_call_target="tpu_custom_call" | custom-call | tf_op jit(solution)/shard_map/total/pallas_call | solution.py:334
  245.1 9.8 add_convert_fusion
  254.9 22.4 %reshape.659 = bf16[6,260,3,12,64]{4,3,2,1,0:T(8,128)(2,1)} reshape(bf16[1560,2304]{1,0:T(8,128)(2,1)} %add_convert_fusion) | data formatting | bytes 14376960 | tf_op jit(solution)/shard_map/reshape | solution.py:511
  277.3 14.4 %fusion.95 = (bf16[6,260,1,12,64]{4,3,2,1,0:T(8,128)(2,1)}, bf16[6,260,1,12,64]{4,3,2,1,0:T(8,128)(2,1)}, bf16[6,260,1,12,64]{4,3,2,1,0:T(8,128)(2,1)}) fusion(bf16[6,260,3,12,64]{4,3,2,1,0:T(8,128)(2,1)} %reshape.659), kind=kLoop, calls=%fused_computation.269 | loop fusion | bytes 14376960 | tf_op jit(solution)/shard_map/slice | solution.py:512
  300.2 10.4 %copy.113 = bf16[6,260,1,12,64]{1,4,3,0,2:T(8,128)(2,1)} copy(bf16[6,260,1,12,64]{4,3,2,1,0:T(8,128)(2,1)} %get-tuple-element.100) | data formatting | bytes 4792320
  310.6 9.5 copy.115
  320.1 15.9 %fusion.24 = f32[6,12,260,260]{2,3,1,0:T(8,128)} fusion(bf16[6,260,1,12,64]{1,4,3,0,2:T(8,128)(2,1)} %copy.115, bf16[6,260,1,12,64]{1,4,3,0,2:T(8,128)(2,1)S(1)} %copy.114), kind=kOutput, calls=%fused_computation.76 | convolution fusion | flops 623001600 | bytes 24261120 | tf_op jit(solution)/shard_map/eqhd,ekhd->ehqk/dot_general | solution.py:515
  336.0 37.4 %fusion.103 = (f32[6,12,260]{2,1,0:T(8,128)}, f32[6,12,260,260]{2,3,1,0:T(8,128)}) fusion(f32[6,12,260,260]{2,3,1,0:T(8,128)} %fusion.24, pred[6,260]{1,0:T(8,128)(4,1)S(1)} %broadcast_compare_fusion), kind=kOutput, calls=%fused_computation.277 | output fusion | flops 29203460 | bytes 39014040 | tf_op jit(solution)/shard_map/sub | solution.py:520
  373.4 11.1 %convert_bitcast_fusion.1 = bf16[6,260,12,64]{1,3,2,0:T(8,128)(2,1)S(1)} fusion(bf16[6,260,1,12,64]{1,4,3,0,2:T(8,128)(2,1)S(1)} %copy-done.14, f32[6,12,260,260]{2,3,1,0:T(8,128)} %get-tuple-element.163, f32[6,12,260]{2,1,0:T(8,128)} %get-tuple-element.162), kind=kOutput, calls=%fused_computation.85 | convolution fusion | flops 633934080 | bytes 24336000 | tf_op jit(solution)/shard_map/ehqk,ekhd->eqhd/dot_general | solution.py:523
  402.4 14.6 %fusion.78 = f32[1560,3072]{1,0:T(8,128)} fusion(bf16[768,3072]{1,0:T(8,128)(2,1)} %bitcast.324, f32[1560,768]{1,0:T(8,128)S(1)} %get-tuple-element.165, f32[768]{0:T(1024)S(1)} %copy-done.82, f32[768]{0:T(1024)S(1)} %copy-done.70, f32[1560]{0:T(1024)S(1)} %fusion.66, f32[1560]{0:T(1024)S(1)} %broadcast_multiply_fusion.1), kind=kOutput, calls=%fused_computation.256 | convolution fusion | flops 7366993920 | bytes 28698816 | tf_op jit(solution)/shard_map/dot_general | solution.py:371
  417.1 17.2 %add_add_fusion.4 = f32[1560,768]{1,0:T(8,128)} fusion(f32[1560,768]{1,0:T(8,128)S(1)} %get-tuple-element.165, bf16[3072,768]{1,0:T(8,128)(2,1)S(1)} %bitcast.329, f32[768]{0:T(1024)S(1)} %copy-done.84, f32[1560,3072]{1,0:T(8,128)} %fusion.78, f32[3072]{0:T(1024)S(1)} %copy-done.74), kind=kOutput, calls=%fused_computation.64 | convolution fusion | flops 7411322880 | bytes 33487872 | tf_op jit(solution)/shard_map/dot_general | solution.py:371
  448.1 29.7 %convert_reduce_fusion.1 = (f32[3072]{0:T(1024)}, bf16[1560,3072]{1,0:T(8,128)(2,1)}) fusion(bf16[1560,768]{1,0:T(8,128)(2,1)} %convert_element_type.430, bf16[3072,768]{1,0:T(8,128)(2,1)} %bitcast.326, f32[1560,3072]{1,0:T(8,128)} %fusion.78, f32[3072]{0:T(1024)S(1)} %copy-done.74), kind=kOutput, calls=%fused_computation.17 | convolution fusion | flops 7490393088 | bytes 35893248 | tf_op jit(solution)/shard_map/dot_general | solution.py:381
  477.8 14.7 %multiply_reduce_fusion.4 = (f32[768]{0:T(1024)}, f32[1560]{0:T(1024)S(1)}, f32[768]{0:T(1024)}, f32[1560,768]{1,0:T(8,128)S(1)}) fusion(f32[1560,768]{1,0:T(8,128)S(1)} %bitcast.259, f32[1560]{0:T(1024)S(1)} %fusion.66, f32[1560]{0:T(1024)S(1)} %broadcast_multiply_fusion.1, f32[768]{0:T(1024)S(1)} %copy-done.70, ...), kind=kOutput, calls=%fused_computation.57 | convolution fusion | flops 7370585088 | bytes 23915808 | tf_op jit(solution)/shard_map/dot_general | solution.py:381
  492.5 14.0 %convolution_convert_fusion.1 = bf16[768,3072]{1,0:T(8,128)(2,1)} fusion(bf16[1560,3072]{1,0:T(8,128)(2,1)} %get-tuple-element.171, f32[1560,768]{1,0:T(8,128)S(1)} %bitcast.259, f32[768]{0:T(1024)S(1)} %copy-done.82, f32[768]{0:T(1024)S(1)} %copy-done.70, f32[1560]{0:T(1024)S(1)} %fusion.66, f32[1560]{0:T(1024)S(1)} %broadcast_multiply_fusion.1), kind=kOutput, calls=%fused_computation.38 | convolution fusion | flops 7369353216 | bytes 19114176 | tf_op jit(solution)/shard_map/dot_general | solution.py:375
  516.1 19.5 %convolution_convert_fusion = bf16[3072,768]{1,0:T(8,128)(2,1)} fusion(f32[1560,768]{1,0:T(8,128)} %reshape.627, f32[1560,3072]{1,0:T(8,128)} %fusion.78, f32[3072]{0:T(1024)S(1)} %copy-done.74), kind=kOutput, calls=%fused_computation.37 | convolution fusion | flops 7412484096 | bytes 28692480 | tf_op jit(solution)/shard_map/dot_general | solution.py:375
  548.3 9.5 copy.87
  557.9 15.3 %convert_bitcast_fusion = bf16[6,260,1,12,64]{1,4,3,0,2:T(8,128)(2,1)} fusion(bf16[6,260,12,64]{1,3,2,0:T(8,128)(2,1)} %copy.87, f32[6,12,260,260]{2,3,1,0:T(8,128)} %get-tuple-element.163, f32[6,12,260]{2,1,0:T(8,128)} %get-tuple-element.162), kind=kOutput, calls=%fused_computation.84 | convolution fusion | flops 633934080 | bytes 24336000 | tf_op jit(solution)/shard_map/ehqk,eqhd->ekhd/dot_general | solution.py:659
  573.1 23.5 %multiply_reduce_fusion = (f32[6,12,260]{2,1,0:T(8,128)}, f32[6,12,260,260]{2,3,1,0:T(8,128)}) fusion(f32[6,12,260,260]{2,3,1,0:T(8,128)} %get-tuple-element.163, f32[6,12,260]{2,1,0:T(8,128)} %get-tuple-element.162, bf16[6,260,12,64]{1,3,2,0:T(8,128)(2,1)} %copy.87, bf16[6,260,1,12,64]{1,4,3,0,2:T(8,128)(2,1)S(1)} %copy-done.15), kind=kOutput, calls=%fused_computation.2 | convolution fusion | flops 637584512 | bytes 43879680 | tf_op jit(solution)/shard_map/eqhd,ekhd->ehqk/dot_general | solution.py:662
  596.6 24.4 %multiply_convert_fusion = bf16[6,12,260,260]{2,3,1,0:T(8,128)(2,1)} fusion(f32[6,12,260,260]{2,3,1,0:T(8,128)} %get-tuple-element.168, f32[6,12,260]{2,1,0:T(8,128)} %get-tuple-element.167, f32[6,12,260,260]{2,3,1,0:T(8,128)} %get-tuple-element.163, f32[6,12,260]{2,1,0:T(8,128)} %get-tuple-element.162), kind=kLoop, calls=%fused_computation.1 | loop fusion | flops 19468800 | bytes 48821760 | tf_op jit(solution)/shard_map/convert_element_type | solution.py:666
  621.1 10.6 %fusion.21 = bf16[6,260,1,12,64]{1,4,3,0,2:T(8,128)(2,1)} fusion(bf16[6,12,260,260]{2,3,1,0:T(8,128)(2,1)} %multiply_convert_fusion, bf16[6,260,1,12,64]{1,4,3,0,2:T(8,128)(2,1)S(1)} %copy-done.2), kind=kOutput, calls=%fused_computation.73 | convolution fusion | flops 625397760 | bytes 14526720 | tf_op jit(solution)/shard_map/ehqk,eqhd->ekhd/dot_general | solution.py:676
  644.8 13.6 %copy.92 = bf16[6,260,3,12,64]{1,0,4,3,2:T(8,128)(2,1)} copy(bf16[6,260,3,12,64]{1,4,3,0,2:T(8,128)(2,1)} %get-tuple-element.83) | data formatting | bytes 14376960 | tf_op jit(solution)/shard_map/stack | solution.py:680
  658.4 19.5 %convert_element_type.435 = bf16[1560,2304]{0,1:T(8,128)(2,1)} reshape(bf16[6,260,3,12,64]{1,0,4,3,2:T(8,128)(2,1)} %copy.92) | data formatting | bytes 14376960 | tf_op jit(solution)/shard_map/convert_element_type | solution.py:680
  678.0 11.7 %convolution_convert_fusion.2 = bf16[768,2304]{1,0:T(8,128)(2,1)} fusion(bf16[1560,768]{1,0:T(8,128)(2,1)S(1)} %copy-done.25, bf16[1560,2304]{0,1:T(8,128)(2,1)} %convert_element_type.435), kind=kOutput, calls=%fused_computation.39 | convolution fusion | flops 5522522112 | bytes 13123584 | tf_op jit(solution)/shard_map/dot_general | solution.py:375
  689.8 13.1 %multiply_reduce_fusion.5 = (f32[768]{0:T(1024)S(1)}, f32[1560]{0:T(1024)S(1)}, f32[768]{0:T(1024)S(1)}, f32[1560,768]{1,0:T(8,128)}) fusion(f32[1560,768]{1,0:T(8,128)S(1)} %bitcast.261, f32[1560]{0:T(1024)S(1)} %copy-done.54, f32[1560]{0:T(1024)S(1)} %copy-done.55, f32[768]{0:T(1024)S(1)} %copy-done.49, bf16[1560,2304]{0,1:T(8,128)(2,1)} %convert_element_type.435, ...), kind=kOutput, calls=%fused_computation.59 | convolution fusion | flops 5530334208 | bytes 20340000 | tf_op jit(solution)/shard_map/dot_general | solution.py:381
  721.3 14.7 %total.13 = f32[78,128]{1,0:T(8,128)} custom-call(f32[78,128]{1,0:T(8,128)} %bitcast.280), custom_call_target="tpu_custom_call" | custom-call | tf_op jit(solution)/shard_map/total/pallas_call | solution.py:334
  760.1 16.6 %total.10 = f32[8,1024]{1,0:T(8,128)} custom-call(f32[8,1024]{1,0:T(8,128)} %select_maximum_fusion.2.x_ref), custom_call_target="tpu_custom_call" | custom-call | tf_op jit(solution)/shard_map/total/pallas_call | solution.py:334
  789.6 14.3 %total.11 = f32[8,1024]{1,0:T(8,128)} custom-call(f32[8,1024]{1,0:T(8,128)} %select_maximum_fusion.1.x_ref), custom_call_target="tpu_custom_call" | custom-call | tf_op jit(solution)/shard_map/total/pallas_call | solution.py:334
  838.5 16.4 %total.12 = f32[8,1024]{1,0:T(8,128)} custom-call(f32[8,1024]{1,0:T(8,128)} %select_maximum_fusion.x_ref), custom_call_target="tpu_custom_call" | custom-call | tf_op jit(solution)/shard_map/total/pallas_call | solution.py:334
  862.6 114.8 %scatter.1 = (f32[32,256]{1,0:T(8,128)}, f32[72,256]{1,0:T(8,128)}, f32[8,1024]{1,0:T(8,128)}, f32[32,768]{1,0:T(8,128)}, f32[24,2304]{1,0:T(8,128)}, /*index=5*...) custom-call(bf16[2,2,4,2,32,256]{5,4,3,2,1,0:T(8,128)(2,1)} %bitcast.265, ...), custom_call_target="tpu_custom_call" | custom-call | tf_op jit(solution)/shard_map/scatter/pallas_call | solution.py:286
  (426 shorter events, 281.8 us)
Async XLA Ops:
  6.9 100.7 %copy-start.35 = (f32[6,64]{1,0:T(8,128)}, f32[6,64]{1,0:T(8,128)S(1)}, u32[]{:S(2)}) copy-start(f32[6,64]{1,0:T(8,128)S(1)} %fusion.67) | copy-start | bytes 4612
  108.5 100.9 %copy-start.66 = (f32[1024]{0:T(1024)}, f32[1024]{0:T(1024)S(1)}, u32[]{:S(2)}) copy-start(f32[1024]{0:T(1024)S(1)} %reshape.645) | copy-start | bytes 12292
  111.2 98.3 %copy-start.68 = (f32[1024]{0:T(1024)}, f32[1024]{0:T(1024)S(1)}, u32[]{:S(2)}) copy-start(f32[1024]{0:T(1024)S(1)} %reshape.646) | copy-start | bytes 12292
  114.4 73.0 %copy-start.87 = (f32[256]{0:T(256)}, f32[256]{0:T(256)S(1)}, u32[]{:S(2)}) copy-start(f32[256]{0:T(256)S(1)} %reshape.643) | copy-start | bytes 3076
  114.6 53.1 %copy-start.62 = (f32[256]{0:T(256)}, f32[256]{0:T(256)S(1)}, u32[]{:S(2)}) copy-start(f32[256]{0:T(256)S(1)} %reshape.641) | copy-start | bytes 3076
  114.8 72.6 %copy-start.89 = (f32[256]{0:T(256)}, f32[256]{0:T(256)S(1)}, u32[]{:S(2)}) copy-start(f32[256]{0:T(256)S(1)} %reshape.644) | copy-start | bytes 3076
  114.9 52.9 %copy-start.64 = (f32[256]{0:T(256)}, f32[256]{0:T(256)S(1)}, u32[]{:S(2)}) copy-start(f32[256]{0:T(256)S(1)} %reshape.642) | copy-start | bytes 3076
  116.5 114.4 %copy-start.48 = (f32[768]{0:T(1024)}, f32[768]{0:T(1024)S(1)}, u32[]{:S(2)}) copy-start(f32[768]{0:T(1024)S(1)} %reshape.648) | copy-start | bytes 9220
  119.9 47.8 %copy-start.4 = (f32[256,1176]{0,1:T(8,128)}, f32[256,1176]{0,1:T(8,128)S(1)}, u32[]{:S(2)}) copy-start(f32[256,1176]{0,1:T(8,128)S(1)} %get-tuple-element.159) | copy-start | bytes 3612676
  140.3 27.5 %copy-start.58 = (f32[1,256]{1,0:T(1,128)}, f32[1,256]{1,0:T(1,128)S(1)}, u32[]{:S(2)}) copy-start(f32[1,256]{1,0:T(1,128)S(1)} %get-tuple-element.87) | copy-start | bytes 3076
  140.3 27.5 %copy-start.60 = (f32[1,256]{1,0:T(1,128)}, f32[1,256]{1,0:T(1,128)S(1)}, u32[]{:S(2)}) copy-start(f32[1,256]{1,0:T(1,128)S(1)} %get-tuple-element.153) | copy-start | bytes 3076
  168.6 18.8 %copy-start.95 = (bf16[2,2,4,2,8,1024]{5,4,3,2,1,0:T(8,128)(2,1)S(1)}, bf16[2,2,4,2,8,1024]{5,4,3,2,1,0:T(8,128)(2,1)}, u32[]{:S(2)}) copy-start(bf16[2,2,4,2,8,1024]{5,4,3,2,1,0:T(8,128)(2,1)} %get-tuple-element.46) | copy-start | bytes 1572868
  170.9 19.9 %copy-start.27 = (f32[1176,256]{1,0:T(8,128)}, f32[1176,256]{1,0:T(8,128)S(1)}, u32[]{:S(2)}) copy-start(f32[1176,256]{1,0:T(8,128)S(1)} %get-tuple-element.160) | copy-start | bytes 3612676
  300.2 19.9 %copy-start.1 = (bf16[6,260,1,12,64]{1,4,3,0,2:T(8,128)(2,1)}, bf16[6,260,1,12,64]{1,4,3,0,2:T(8,128)(2,1)S(1)}, u32[]{:S(2)}) copy-start(bf16[6,260,1,12,64]{1,4,3,0,2:T(8,128)(2,1)S(1)} %copy.114) | copy-start | bytes 7188484
  336.0 37.4 %copy-start.14 = (bf16[6,260,1,12,64]{1,4,3,0,2:T(8,128)(2,1)S(1)}, bf16[6,260,1,12,64]{1,4,3,0,2:T(8,128)(2,1)}, u32[]{:S(2)}) copy-start(bf16[6,260,1,12,64]{1,4,3,0,2:T(8,128)(2,1)} %copy.113) | copy-start | bytes 7188484
  395.5 21.5 %slice-start.12 = ((s8[4718592]{0:T(1024)(128)(4,1)}), s8[4194304]{0:T(1024)(128)(4,1)S(1)}, s32[]{:S(2)}) async-start(s8[4718592]{0:T(1024)(128)(4,1)} %bitcast.327), calls=%async_computation.12 | async-start | bytes 8388608
  446.0 31.8 %slice-start.8 = ((s8[4792320]{0:T(1024)(128)(4,1)}), s8[598016]{0:T(1024)(128)(4,1)S(1)}, s32[]{:S(2)}) async-start(s8[4792320]{0:T(1024)(128)(4,1)} %bitcast.258), calls=%async_computation.8 | async-start | bytes 1196032
  448.1 29.7 %slice-start.9 = ((s8[4792320]{0:T(1024)(128)(4,1)}), s8[4194304]{0:T(1024)(128)(4,1)S(1)}, s32[]{:S(2)}) async-start(s8[4792320]{0:T(1024)(128)(4,1)} %bitcast.258), calls=%async_computation.9 | async-start | bytes 8388608
  510.4 25.2 %copy-start.42 = (f32[1560]{0:T(1024)}, f32[1560]{0:T(1024)S(1)}, u32[]{:S(2)}) copy-start(f32[1560]{0:T(1024)S(1)} %negate_multiply_fusion.1) | copy-start | bytes 18724
  510.4 25.2 %slice-start = ((s8[4792320]{0:T(1024)(128)(4,1)}), s8[598016]{0:T(1024)(128)(4,1)S(1)}, s32[]{:S(2)}) async-start(s8[4792320]{0:T(1024)(128)(4,1)} %bitcast.250), calls=%async_computation | async-start | bytes 1196032
  516.1 19.6 %slice-start.1 = ((s8[4792320]{0:T(1024)(128)(4,1)}), s8[4194304]{0:T(1024)(128)(4,1)S(1)}, s32[]{:S(2)}) async-start(s8[4792320]{0:T(1024)(128)(4,1)} %bitcast.250), calls=%async_computation.1 | async-start | bytes 8388608
  516.1 19.6 %copy-start = (f32[1560,768]{1,0:T(8,128)S(1)}, f32[1560,768]{1,0:T(8,128)}, u32[]{:S(2)}) copy-start(f32[1560,768]{1,0:T(8,128)} %reshape.627) | copy-start | bytes 14376964
  596.6 24.4 %copy-start.2 = (bf16[6,260,1,12,64]{1,4,3,0,2:T(8,128)(2,1)S(1)}, bf16[6,260,1,12,64]{1,4,3,0,2:T(8,128)(2,1)}, u32[]{:S(2)}) copy-start(bf16[6,260,1,12,64]{1,4,3,0,2:T(8,128)(2,1)} %copy-done.1) | copy-start | bytes 7188484
  658.4 19.5 %copy-start.25 = (bf16[1560,768]{1,0:T(8,128)(2,1)S(1)}, bf16[1560,768]{1,0:T(8,128)(2,1)}, u32[]{:S(2)}) copy-start(bf16[1560,768]{1,0:T(8,128)(2,1)} %copy-done.24) | copy-start | bytes 7188484
  658.4 31.3 %slice-start.10 = ((s8[4792320]{0:T(1024)(128)(4,1)}), s8[598016]{0:T(1024)(128)(4,1)S(1)}, s32[]{:S(2)}) async-start(s8[4792320]{0:T(1024)(128)(4,1)} %bitcast.260), calls=%async_computation.10 | async-start | bytes 1196032
  677.9 28.9 %slice-start.2 = ((s8[4792320]{0:T(1024)(128)(4,1)}), s8[4194304]{0:T(1024)(128)(4,1)S(1)}, s32[]{:S(2)}) async-start(s8[4792320]{0:T(1024)(128)(4,1)} %bitcast.252), calls=%async_computation.2 | async-start | bytes 8388608
  677.9 28.9 %slice-start.4 = ((s8[4792320]{0:T(1024)(128)(4,1)}), s8[4194304]{0:T(1024)(128)(4,1)S(1)}, s32[]{:S(2)}) async-start(s8[4792320]{0:T(1024)(128)(4,1)} %bitcast.254), calls=%async_computation.4 | async-start | bytes 8388608
  718.0 33.2 %slice-start.6 = ((s8[4816896]{0:T(1024)(128)(4,1)}), s8[622592]{0:T(1024)(128)(4,1)S(1)}, s32[]{:S(2)}) async-start(s8[4816896]{0:T(1024)(128)(4,1)} %bitcast.256), calls=%async_computation.6 | async-start | bytes 1245184
  751.3 27.5 %copy-start.72 = (f32[1,1024]{1,0:T(1,128)S(1)}, f32[1,1024]{1,0:T(1,128)}, u32[]{:S(2)}) copy-start(f32[1,1024]{1,0:T(1,128)} %get-tuple-element.92) | copy-start | bytes 12292
  786.1 19.2 %copy-start.77 = (f32[1,256]{1,0:T(1,128)S(1)}, f32[1,256]{1,0:T(1,128)}, u32[]{:S(2)}) copy-start(f32[1,256]{1,0:T(1,128)} %get-tuple-element.89) | copy-start | bytes 3076
  833.9 23.0 %copy-start.76 = (f32[1,256]{1,0:T(1,128)S(1)}, f32[1,256]{1,0:T(1,128)}, u32[]{:S(2)}) copy-start(f32[1,256]{1,0:T(1,128)} %get-tuple-element.86) | copy-start | bytes 3076
  833.9 23.4 %copy-start.31 = (bf16[2,2,4,2,32,256]{5,4,3,2,1,0:T(8,128)(2,1)S(1)}, bf16[2,2,4,2,32,256]{5,4,3,2,1,0:T(8,128)(2,1)}, u32[]{:S(2)}) copy-start(bf16[2,2,4,2,32,256]{5,4,3,2,1,0:T(8,128)(2,1)} %get-tuple-element.43) | copy-start | bytes 1572868
  (79 other events, 483.0 us)

commit v2 on v1

v2 whole, which is shorter than its diff:
```python
import functools

import jax
import jax.numpy as jnp
from jax import lax
from jax.experimental import pallas as pl
from jax.experimental.pallas import tpu as pltpu
from jax.sharding import PartitionSpec as P
MESH = pl.DeviceIdType.MESH
DMA = pltpu.SemaphoreType.DMA


def rcopy(src, dst, send, recv, dev):
    return pltpu.make_async_remote_copy(
        src_ref=src, dst_ref=dst, send_sem=send, recv_sem=recv, device_id=dev, device_id_type=MESH
    )


class Place:
    def __init__(self, A, B):
        self.A, self.B, self.A2, self.Z = A, B, A // 2, B // 2
        a, b = lax.axis_index("dp"), lax.axis_index("fsdp")
        self.a, self.b = a, b
        self.y, self.x = a // 2, lax.rem(a, 2)
        self.z, self.c = b // 2, lax.rem(b, 2)
        self.zs = [lax.rem(self.z + k, self.Z) for k in range(1, self.Z)]
        self.ys = [lax.rem(self.y + k, self.A2) for k in range(1, self.A2)]
        self.zfrom = [lax.rem(self.z + self.Z - k, self.Z) for k in range(1, self.Z)]
        self.yfrom = [lax.rem(self.y + self.A2 - k, self.A2) for k in range(1, self.A2)]
        self.me = (a, b)
        self.core = (a, self.z * 2 + 1 - self.c)
        self.xpeer = (self.y * 2 + 1 - self.x, b)
        self.c1, self.x1 = 1 - self.c, 1 - self.x
        self.dpeers = [(lax.rem(a + k, A), b) for k in range(1, A)]
        self.zpeers = [(a, zz * 2 + self.c) for zz in self.zs]
        self.ypeers = [(yy * 2 + self.x, b) for yy in self.ys]

        self.bpeers = [(a, lax.rem(b + k, B)) for k in range(1, B)]

    def greet(self, totals=True):
        peers = self.dpeers + self.bpeers if totals else self.zpeers + self.ypeers + [self.xpeer, self.core]
        bar = pltpu.get_barrier_semaphore()
        for p in peers:
            pl.semaphore_signal(bar, inc=1, device_id=p, device_id_type=MESH)
        pl.semaphore_wait(bar, len(peers))


class GatherItem:
    def __init__(self, pc, i, cols, order, src, out, sems):
        self.pc, self.order, self.src_ref, self.out = pc, order, src, out
        self.cols = slice(None) if cols is None else pl.ds(*cols)
        self.loc, self.s1, self.r1, self.s2, self.r2, self.s3, self.r3, self.sc, self.rc = [s.at[i] for s in sems]
        self.here = False
        p = pc
        every = slice(None)
        self.got2 = [(p.y, p.x1)] if order == 0 else [(yy, p.x) for yy in p.yfrom]
        self.got3 = [(yy, every) for yy in p.yfrom] if order == 0 else [(every, p.x1)]
        self.to2 = [p.xpeer] if order == 0 else p.ypeers
        self.to3 = p.ypeers if order == 0 else [p.xpeer]
        self.crossed = [(p.y, p.x)] + self.got2 + self.got3

    def src(self):
        return self.src_ref.at[:, self.cols]

    def block(self, y, x, z, c):
        return self.out.at[y, x, z, c, :, self.cols]

    def local(self):
        p = self.pc
        return pltpu.make_async_copy(self.src(), self.block(p.y, p.x, p.z, p.c), self.loc)

    def send1(self, k):
        p = self.pc
        return rcopy(self.src(), self.block(p.y, p.x, p.z, p.c), self.s1.at[k], self.r1.at[k], p.zpeers[k])

    def send2(self, k):
        p = self.pc
        col = self.block(p.y, p.x, slice(None), p.c)
        return rcopy(col, col, self.s2.at[k], self.r2.at[k], self.to2[k])

    def send3(self, k):
        p, every = self.pc, slice(None)
        blk = self.block(p.y, every, every, p.c) if self.order == 0 else self.block(every, p.x, every, p.c)
        return rcopy(blk, blk, self.s3.at[k], self.r3.at[k], self.to3[k])

    def cross(self, j, c):
        blk = self.block(*self.crossed[j], slice(None), c)
        return rcopy(blk, blk, self.sc.at[j], self.rc.at[j], self.pc.core)

    def wait(self, got, send, recv):
        rcopy(got, got, send, recv, self.pc.me).wait_recv()

    def start(self):
        self.local().start()
        for k in range(len(self.pc.zpeers)):
            self.send1(k).start()

    def second(self):
        p = self.pc
        self.local().wait()
        for k, zz in enumerate(p.zfrom):
            self.wait(self.block(p.y, p.x, zz, p.c), self.s1.at[k], self.r1.at[k])
        for k in range(len(self.to2)):
            self.send2(k).start()
        self.cross(0, p.c).start()

    def third(self):
        p = self.pc
        for k, (yy, xx) in enumerate(self.got2):
            self.wait(self.block(yy, xx, slice(None), p.c), self.s2.at[k], self.r2.at[k])
        for k in range(len(self.to3)):
            self.send3(k).start()
        for k in range(len(self.got2)):
            self.cross(1 + k, p.c).start()

    def fourth(self):
        p = self.pc
        for k, (yy, xx) in enumerate(self.got3):
            self.wait(self.block(yy, xx, slice(None), p.c), self.s3.at[k], self.r3.at[k])
            self.cross(1 + len(self.got2) + k, p.c).start()

    def arrived(self):
        if self.here:
            return
        self.here = True
        for j in range(len(self.crossed)):
            self.cross(j, self.pc.c1).wait_recv()

    def drain(self):
        for k in range(len(self.pc.zpeers)):
            self.send1(k).wait_send()
        for k in range(len(self.to2)):
            self.send2(k).wait_send()
        for k in range(len(self.to3)):
            self.send3(k).wait_send()
        for j in range(len(self.crossed)):
            self.cross(j, self.pc.c).wait_send()


def gather_sems(A, B, n):
    A2, Z = A // 2, B // 2
    m = max(A2 - 1, 1)
    return [DMA((n,)), DMA((n, Z - 1)), DMA((n, Z - 1)), DMA((n, m)), DMA((n, m)), DMA((n, m)), DMA((n, m)), DMA((n, A2 + 1)), DMA((n, A2 + 1))]


def wave(items, lags, stages, hooks=None):
    hooks = hooks or {}
    last = max([len(items) + lags[-1]] + [t + 1 for t in hooks])
    for t in range(last):
        for lag, stage in zip(reversed(lags), reversed(stages)):
            if 0 <= t - lag < len(items):
                getattr(items[t - lag], stage)()
        for hook in hooks.get(t, ()):
            hook()


def wave_stages(items, lags, stages):
    out = []
    for t in range(len(items) + lags[-1]):
        for lag, stage in zip(reversed(lags), reversed(stages)):
            if 0 <= t - lag < len(items):
                out.append(getattr(items[t - lag], stage))
    return out


def cut(widths_parts):
    items, order = [], 0
    for i, (width, parts) in enumerate(widths_parts):
        for q in range(parts):
            items.append((i, None if parts == 1 else (q * (width // parts), width // parts), order))
            order = 1 - order
    return items


class ScatterItem:
    def __init__(self, pc, i, order, src, out, own, r0, r1, r2, r3, sems, cols=None):
        self.pc, self.order, self.src, self.out = pc, order, src, out
        self.cols = slice(None) if cols is None else pl.ds(*cols)
        self.own, self.r0, self.r1, self.r2, self.r3 = own, r0, r1, r2, r3
        self.loc, self.s0, self.q0, self.s1, self.q1, self.s2, self.q2, self.s3, self.q3 = [s.at[i] for s in sems]
        self.sends = []

    def go(self, copy):
        copy().start()
        self.sends.append(copy)

    def start(self):
        p = self.pc
        self.go(lambda: rcopy(self.src.at[:, :, :, p.c1, :, self.cols], self.r0, self.s0, self.q0, p.core))
        self.local().start()

    def local(self):
        return pltpu.make_async_copy(self.src.at[:, :, :, self.pc.c, :, self.cols], self.own, self.loc)

    def add(self, dst, others, lead):
        total = 1
        for d in lead:
            total *= d

        def body(t, _):
            idx, rest = [], t
            for d in reversed(lead):
                idx.append(lax.rem(rest, d))
                rest = rest // d
            idx = tuple(reversed(idx))
            v = dst[idx].astype(jnp.float32)
            for o in others:
                v = v + o[idx].astype(jnp.float32)
            dst[idx] = v.astype(jnp.bfloat16)
            return 0

        lax.fori_loop(0, total, body, 0)

    def second(self):
        p = self.pc
        self.local().wait()
        rcopy(self.r0, self.r0, self.s0, self.q0, p.me).wait_recv()
        self.add(self.own, [self.r0], (p.A2, 2, p.Z))
        if self.order == 0:
            self.go(lambda: rcopy(self.own.at[:, p.x1], self.r1.at[0], self.s1.at[0], self.q1.at[0], p.xpeer))
        else:
            for k, yy in enumerate(p.ys):
                self.go(lambda k=k, yy=yy: rcopy(self.own.at[yy], self.r1.at[k], self.s1.at[k], self.q1.at[k], p.ypeers[k]))

    def third(self):
        p = self.pc
        n1 = 1 if self.order == 0 else p.A2 - 1
        for k in range(n1):
            rcopy(self.r1.at[k], self.r1.at[k], self.s1.at[k], self.q1.at[k], p.me).wait_recv()
        mine = self.own.at[:, p.x] if self.order == 0 else self.own.at[p.y]
        self.add(mine, [self.r1.at[k] for k in range(n1)], (p.A2 if self.order == 0 else 2, p.Z))
        if self.order == 0:
            for k, yy in enumerate(p.ys):
                self.go(lambda k=k, yy=yy: rcopy(self.own.at[yy, p.x], self.r2.at[k], self.s2.at[k], self.q2.at[k], p.ypeers[k]))
        else:
            self.go(lambda: rcopy(self.own.at[p.y, p.x1], self.r2.at[0], self.s2.at[0], self.q2.at[0], p.xpeer))

    def fourth(self):
        p = self.pc
        n2 = p.A2 - 1 if self.order == 0 else 1
        for k in range(n2):
            rcopy(self.r2.at[k], self.r2.at[k], self.s2.at[k], self.q2.at[k], p.me).wait_recv()
        self.add(self.own.at[p.y, p.x], [self.r2.at[k] for k in range(n2)], (p.Z,))
        for k, zz in enumerate(p.zs):
            self.go(lambda k=k, zz=zz: rcopy(self.own.at[p.y, p.x, zz], self.r3.at[k], self.s3.at[k], self.q3.at[k], p.zpeers[k]))

    def arrived(self):
        p = self.pc
        for k in range(p.Z - 1):
            rcopy(self.r3.at[k], self.r3.at[k], self.s3.at[k], self.q3.at[k], p.me).wait_recv()
        v = self.own[p.y, p.x, p.z].astype(jnp.float32)
        for k in range(p.Z - 1):
            v = v + self.r3[k].astype(jnp.float32)
        self.out[:, self.cols] = v[: self.out.shape[0]]

    def drain(self):
        for copy in self.sends:
            copy().wait_send()


def scatter_sems(A, B, n):
    m, Z = max(A // 2 - 1, 1), B // 2
    return [DMA((n,)), DMA((n,)), DMA((n,)), DMA((n, m)), DMA((n, m)), DMA((n, m)), DMA((n, m)), DMA((n, Z - 1)), DMA((n, Z - 1))]


def scatter_scratch(A, B, shape, order):
    A2, Z = A // 2, B // 2
    n1 = (1, A2, Z) if order == 0 else (A2 - 1, 2, Z)
    n2 = (A2 - 1, Z) if order == 0 else (1, Z)
    return [pltpu.VMEM(s + shape, jnp.bfloat16) for s in ((A2, 2, Z), (A2, 2, Z), n1, n2, (Z - 1,))]


def scatter_items(pc, cuts, srcs, outs, bufs, sems, base=0):
    return [ScatterItem(pc, base + j, o, srcs[i], outs[i], *bufs[5 * j : 5 * j + 5], sems, cols) for j, (i, cols, o) in enumerate(cuts)]


def scatter_buffers(A, B, cuts, shapes):
    out = []
    for i, cols, order in cuts:
        out += scatter_scratch(A, B, (shapes[i][0], shapes[i][1] if cols is None else cols[1]), order)
    return out


def split_rows(A, B, g):
    return g.reshape((A // 2, 2, B // 2, 2, g.shape[0] // (A * B), g.shape[1]))


HEAD_DIM = 64
GRID = 14
ln_eps = 1e-06
bn_eps = 1e-05
gelu_coef = 0.7978845608028654
gelu_cube = gelu_coef * 0.044715
bf16, f32 = jnp.bfloat16, jnp.float32
PATCH_PAD = 208


def dot(left, right):
    return jnp.dot(left, right, preferred_element_type=f32)


def dot_nt(left, right):
    return lax.dot_general(left, right, (((1,), (1,)), ((), ())), preferred_element_type=f32)


def dot_tn(left, right):
    return lax.dot_general(left, right, (((0,), (0,)), ((), ())), preferred_element_type=f32)


def smooth(v):
    return (0.5 * v) * (1.0 + jnp.tanh(v * (gelu_coef + gelu_cube * (v * v))))


def smooth_both(v):
    sq = v * v
    t = jnp.tanh(v * (gelu_coef + gelu_cube * sq))
    half = 0.5 * v
    up = 1.0 + t
    return half * up, 0.5 * up + half * ((1.0 - t * t) * (gelu_coef + 3.0 * gelu_cube * sq))


def ln_parts(v):
    center = v - jnp.mean(v, -1, keepdims=True)
    inv = lax.rsqrt(jnp.mean(center * center, -1, keepdims=True) + ln_eps)
    return center * inv, inv


def ln_back(dy, hat, inv, gain):
    dh = dy * gain
    return inv * (dh - jnp.mean(dh, -1, keepdims=True) - hat * jnp.mean(dh * hat, -1, keepdims=True))


def colsum(v):
    return jnp.sum(v, 0, keepdims=True)


def iota(shape, dim):
    return lax.broadcasted_iota(jnp.int32, shape, dim)


def valid_of(position, length, patches):
    text = position - PATCH_PAD
    return jnp.where((position < patches) | ((text >= 0) & (text < length)), 1.0, 0.0).astype(f32)


def spread(rows, patches, seq):
    i, j = iota((rows, seq), 0), iota((rows, seq), 1)
    hit = ((i < patches) & (j == i)) | ((i >= PATCH_PAD) & (j == i - (PATCH_PAD - patches)))
    return jnp.where(hit, 1.0, 0.0).astype(bf16)


def gather_rows(seq, rows, patches):
    j, i = iota((seq, rows), 0), iota((seq, rows), 1)
    hit = ((i < patches) & (j == i)) | ((i >= PATCH_PAD) & (j == i - (PATCH_PAD - patches)))
    return jnp.where(hit, 1.0, 0.0).astype(bf16)


def lane_masks(width):
    lane = iota((1, 2 * width), 1)
    low = jnp.where(lane < width, 1.0, 0.0).astype(bf16)
    return low, (1.0 - low.astype(f32)).astype(bf16)


class Plan:
    def __init__(self, step, steps, points, stages):
        self.step, self.steps, self.points = step, steps, points
        total, n = steps * points, len(stages)
        self.due = [stages[n * q // total : n * (q + 1) // total] for q in range(total)]

    def __call__(self, point):
        for s in range(self.steps):
            stages = self.due[s * self.points + point]
            if stages:

                @pl.when(self.step == s)
                def _():
                    for stage in stages:
                        stage()


def attend_kernel(n, patches, len_ref, act, text, wp, wqkv, wout, params, x_o, h1_o, qkv_o, o_o, x2_o, h2_o):
    width = text.shape[2]
    slots = text.shape[1]
    rows = PATCH_PAD + slots
    step = pl.program_id(0)
    lows = lane_masks(HEAD_DIM)
    bp, g1, b1, bo, g2, b2 = (params[v : v + 1, :width] for v in (6, 7, 8, 10, 11, 12))
    bqkv = jnp.concatenate([params[9:10, :width], jnp.zeros((1, width), f32), params[9:10, width : 2 * width]], 1)
    patch = dot(act[...].reshape(n * PATCH_PAD, act.shape[2]), wp[...]) + bp
    for i in range(n):
        length = len_ref[step * n + i]
        keep = jnp.where(iota((slots, 1), 0) < length, 1.0, 0.0).astype(f32)
        x_o[i * rows : i * rows + PATCH_PAD] = patch[i * PATCH_PAD : (i + 1) * PATCH_PAD]
        x_o[i * rows + PATCH_PAD : (i + 1) * rows] = text[i].astype(f32) * keep
    hat, _ = ln_parts(x_o[...])
    h1 = (hat * g1 + b1).astype(bf16)
    h1_o[...] = h1
    qkv_o[...] = (dot(h1, wqkv[...]) + bqkv).astype(bf16)
    for i in range(n):
        at = slice(i * rows, (i + 1) * rows)
        bias = jnp.where(valid_of(iota((1, rows), 1), len_ref[step * n + i], patches) > 0.5, 0.0, -1e30)
        for j in range(width // (2 * HEAD_DIM)):
            cols = [slice(p * width + j * 128, p * width + (j + 1) * 128) for p in range(3)]
            q = qkv_o[at, cols[0]] * bf16(HEAD_DIM**-0.5)
            k, v = qkv_o[at, cols[1]], qkv_o[at, cols[2]]
            mixed = 0.0
            for low in lows:
                s = dot_nt(q * low, k) + bias
                e = jnp.exp(s - jnp.max(s, -1, keepdims=True))
                pr = (e * (1.0 / jnp.sum(e, -1, keepdims=True))).astype(bf16)
                mixed = mixed + dot(pr, v * low)
            o_o[at, cols[0]] = mixed.astype(bf16)
    x2 = x_o[...] + dot(o_o[...], wout[...]) + bo
    x2_o[...] = x2
    hat2, _ = ln_parts(x2)
    h2_o[...] = (hat2 * g2 + b2).astype(bf16)


def whole(shape):
    return pl.BlockSpec(shape, lambda *_: (0,) * len(shape), pipeline_mode=pl.Buffered(1))


def attend(lengths, act, text, wp, wqkv, wout, params, patches, n):
    examples, slots, width = text.shape
    rows = PATCH_PAD + slots
    steps = examples // n
    blk = lambda w: pl.BlockSpec((n * rows, w), lambda s: (s, 0))
    out = lambda w, t: jax.ShapeDtypeStruct((examples * rows, w), t)
    return pl.pallas_call(
        functools.partial(attend_kernel, n, patches),
        grid=(steps,),
        out_shape=[out(width, f32), out(width, bf16), out(3 * width, bf16), out(width, bf16), out(width, f32), out(width, bf16)],
        in_specs=[
            pl.BlockSpec(memory_space=pltpu.SMEM),
            pl.BlockSpec((n,) + act.shape[1:], lambda s: (s, 0, 0)),
            pl.BlockSpec((n,) + text.shape[1:], lambda s: (s, 0, 0)),
        ]
        + [whole(w.shape) for w in (wp, wqkv, wout, params)],
        out_specs=[blk(width), blk(width), blk(3 * width), blk(width), blk(width), blk(width)],
        compiler_params=pltpu.CompilerParams(vmem_limit_bytes=56 << 20),
        name="attend",
    )(lengths, act, text, wp, wqkv, wout, params)


def ffn_kernel(n, patches, len_ref, h2, x2_h, cot, wu, bu, wd, params, out_h, dx2_h, gup, gdown, gbu, small, g_s, h2t, acc, dh, m_s, du_s, x2, out, sems):
    c, last = pl.program_id(0), pl.num_programs(0) - 1
    examples, seq, width = cot.shape
    rows = PATCH_PAD + seq - patches
    blocks = examples // n
    load = pltpu.make_async_copy(x2_h, x2, sems.at[0, 0])

    def leave(i, at):
        return pltpu.make_async_copy(out.at[i], out_h.at[i], sems.at[1, i]), pltpu.make_async_copy(dh.at[at], dx2_h.at[at], sems.at[2, i])

    @pl.when(c == 0)
    def _():
        load.start()

        def body(i, _):
            at = pl.ds(pl.multiple_of(i * rows, 16), rows)
            valid = valid_of(iota((rows, 1), 0), len_ref[i], patches)
            g_s[at] = (dot(spread(rows, patches, seq), cot[i]) * valid).astype(bf16)
            acc[at] = jnp.zeros((rows, width), f32)
            dh[at] = jnp.zeros((rows, width), f32)
            return 0

        lax.fori_loop(0, examples, body, 0)
        h2t[...] = h2[...].T

    def block(r, sums):
        at = pl.ds(pl.multiple_of(r * (n * rows), 16), n * rows)
        m, slope = smooth_both(dot(h2[at], wu[...]) + bu[13:14])
        m = m.astype(bf16)
        m_s[at] = m
        acc[at] += dot(m, wd[...])
        du = dot_nt(g_s[at], wd[...]) * slope
        sums = sums + colsum(du)
        du = du.astype(bf16)
        du_s[at] = du
        dh[at] += dot_nt(du, wu[...])
        return sums

    gbu[...] = lax.fori_loop(0, blocks, block, jnp.zeros(gbu.shape, f32), unroll=True)
    gup[...] = dot(h2t[...], du_s[...]).astype(bf16)
    gdown[...] = dot_tn(m_s[...], g_s[...]).astype(bf16)

    @pl.when(c == last)
    def _():
        load.wait()

        def body(i, sums):
            at = pl.ds(pl.multiple_of(i * rows, 16), rows)
            valid = valid_of(iota((rows, 1), 0), len_ref[i], patches)
            result = (acc[at] + x2[at] + params[14:15, :width]) * valid
            out[i] = dot(gather_rows(seq, rows, patches), result.astype(bf16)).astype(bf16)
            hat, inv = ln_parts(x2[at])
            g = g_s[at].astype(f32)
            dy = dh[at]
            dh[at] = g + ln_back(dy, hat, inv, params[11:12, :width])
            for copy in leave(i, at):
                copy.start()
            return sums[0] + colsum(g), sums[1] + colsum(dy * hat), sums[2] + colsum(dy)

        zero = jnp.zeros((1, width), f32)
        a, b, d = lax.fori_loop(0, examples, body, (zero, zero, zero))
        small[0:1], small[1:2], small[2:3] = a, b, d
        small[3:8] = jnp.zeros((5, width), f32)

        def wait(i, _):
            for copy in leave(i, pl.ds(pl.multiple_of(i * rows, 16), rows)):
                copy.wait()
            return 0

        lax.fori_loop(0, examples, wait, 0)


def ffn(lengths, h2, x2, cot, wu, wd, params, patches, n, chunk):
    examples, seq, width = cot.shape
    total, hidden = h2.shape[0], wu.shape[1]
    col = lambda rows: pl.BlockSpec((rows, chunk), lambda c: (0, c))
    row = pl.BlockSpec((chunk, width), lambda c: (c, 0))
    return pl.pallas_call(
        functools.partial(ffn_kernel, n, patches),
        grid=(hidden // chunk,),
        out_shape=[
            jax.ShapeDtypeStruct(cot.shape, bf16),
            jax.ShapeDtypeStruct((total, width), f32),
            jax.ShapeDtypeStruct((width, hidden), bf16),
            jax.ShapeDtypeStruct((hidden, width), bf16),
            jax.ShapeDtypeStruct((1, hidden), f32),
            jax.ShapeDtypeStruct((8, width), f32),
        ],
        in_specs=[pl.BlockSpec(memory_space=pltpu.SMEM), whole(h2.shape), pl.BlockSpec(memory_space=pl.ANY), whole(cot.shape), col(width), col(params.shape[0]), row, whole(params.shape)],
        out_specs=[pl.BlockSpec(memory_space=pl.ANY), pl.BlockSpec(memory_space=pl.ANY), col(width), row, col(1), whole((8, width))],
        scratch_shapes=[
            pltpu.VMEM((total, width), bf16),
            pltpu.VMEM((width, total), bf16),
            pltpu.VMEM((total, width), f32),
            pltpu.VMEM((total, width), f32),
            pltpu.VMEM((total, chunk), bf16),
            pltpu.VMEM((total, chunk), bf16),
            pltpu.VMEM((total, width), f32),
            pltpu.VMEM(cot.shape, bf16),
            DMA((3, examples)),
        ],
        compiler_params=pltpu.CompilerParams(vmem_limit_bytes=60 << 20),
        name="ffn",
    )(lengths, h2, x2, cot, wu, params, wd, params)


def attend_back_kernel(A, B, n, patches, slots, cuts, n_sc, *refs):
    (len_ref, dx2, x, h1, qkv, o, act, wp, wqkv, wout, params), refs = refs[:11], refs[11:]
    srcs, refs = refs[:n_sc], refs[n_sc:]
    (dact, gtext, gqkv, gout, gpatch, small, small3), refs = refs[:7], refs[7:]
    sums, refs = refs[:n_sc], refs[n_sc:]
    (aqkv, aout, apatch, do_s, dq_s), refs = refs[:5], refs[5:]
    step, last = pl.program_id(0), pl.num_programs(0) - 1
    width = x.shape[1]
    g1 = params[7:8, :width]
    rows = PATCH_PAD + slots
    lows = lane_masks(HEAD_DIM)
    scale = bf16(HEAD_DIM**-0.5)

    @pl.when(step == 0)
    def _():
        for ref in (aqkv, aout, apatch, small, small3):
            ref[...] = jnp.zeros(ref.shape, f32)

    moves, stages = [], []
    if n_sc:
        pc = Place(A, B)
        pl.when(step == 0)(lambda: pc.greet(False))
        moves = scatter_items(pc, cuts, srcs, sums, refs[: 5 * len(cuts)], refs[5 * len(cuts) :])
        stages = wave_stages(moves, (0, 2, 5, 8, 11), ["start", "second", "third", "fourth", "arrived"])
    progress = Plan(step, 6, 3, stages)
    progress(0)
    db = dx2[...].astype(bf16)
    do_s[...] = dot_nt(db, wout[...]).astype(bf16)
    aout[...] += dot_tn(o[...], db)
    for i in range(n):
        at = slice(i * rows, (i + 1) * rows)
        bias = jnp.where(valid_of(iota((rows, 1), 0), len_ref[step * n + i], patches) > 0.5, 0.0, -1e30)
        for j in range(width // (2 * HEAD_DIM)):
            cols = [slice(p * width + j * 128, p * width + (j + 1) * 128) for p in range(3)]
            q, k, v = qkv[at, cols[0]] * scale, qkv[at, cols[1]], qkv[at, cols[2]]
            ks = k * scale
            do = do_s[at, cols[0]]
            dq = dk = dv = 0.0
            for low in lows:
                s = dot_nt(k * low, q) + bias
                e = jnp.exp(s - jnp.max(s, 0, keepdims=True))
                p = e * (1.0 / jnp.sum(e, 0, keepdims=True))
                dv = dv + dot(p.astype(bf16), do * low)
                dp = dot_nt(v * low, do)
                ds = (p * (dp - jnp.sum(p * dp, 0, keepdims=True))).astype(bf16)
                dk = dk + dot(ds, q * low)
                dq = dq + dot_tn(ds, ks * low)
            dq_s[at, cols[0]], dq_s[at, cols[1]], dq_s[at, cols[2]] = dq.astype(bf16), dk.astype(bf16), dv.astype(bf16)
    progress(1)
    aqkv[...] += dot_tn(h1[...], dq_s[...])
    dh1 = dot_nt(dq_s[...], wqkv[...])
    hat, inv = ln_parts(x[...])
    dx = dx2[...] + ln_back(dh1, hat, inv, g1)
    progress(2)
    dps = []
    for i in range(n):
        keep = jnp.where(iota((slots, 1), 0) < len_ref[step * n + i], 1.0, 0.0).astype(f32)
        gtext[i] = (dx[i * rows + PATCH_PAD : (i + 1) * rows] * keep).astype(bf16)
        inside = iota((PATCH_PAD, 1), 0) < patches
        dps.append(jnp.where(inside, dx[i * rows : i * rows + PATCH_PAD], 0.0).astype(bf16))
    dp = jnp.concatenate(dps, 0)
    dact[...] = dot_nt(dp, wp[...]).reshape(dact.shape)
    apatch[...] += dot_tn(act[...].reshape(n * PATCH_PAD, act.shape[2]), dp)
    small[0:1] += colsum(dh1 * hat)
    small[1:2] += colsum(dh1)
    small[2:3] += colsum(db.astype(f32))
    small[3:4] += colsum(dp.astype(f32))
    small3[0:1] += colsum(dq_s[...].astype(f32))

    @pl.when(step == last)
    def _():
        for m in moves:
            m.drain()
        gqkv[...], gout[...], gpatch[...] = aqkv[...].astype(bf16), aout[...].astype(bf16), apatch[...].astype(bf16)


def attend_back(A, B, lengths, dx2, x, h1, qkv, o, act, wp, wqkv, wout, params, grads, parts, slots, patches, n, cid):
    examples, _, channels = act.shape
    width = x.shape[1]
    rows = PATCH_PAD + slots
    blk = lambda w: pl.BlockSpec((n * rows, w), lambda s: (s, 0))
    assert examples == 6 * n
    cuts = cut([(g.shape[1], q) for g, q in zip(grads, parts)])
    shapes = [(g.shape[0] // (A * B), g.shape[1]) for g in grads]
    hbm = pl.BlockSpec(memory_space=pl.ANY)
    remote = dict(collective_id=cid, has_side_effects=True) if grads else {}
    cube = lambda a, b: pl.BlockSpec((n, a, b), lambda s: (s, 0, 0))
    return pl.pallas_call(
        functools.partial(attend_back_kernel, A, B, n, patches, slots, cuts, len(grads)),
        grid=(examples // n,),
        out_shape=[
            jax.ShapeDtypeStruct(act.shape, f32),
            jax.ShapeDtypeStruct((examples, slots, width), bf16),
            jax.ShapeDtypeStruct(wqkv.shape, bf16),
            jax.ShapeDtypeStruct(wout.shape, bf16),
            jax.ShapeDtypeStruct(wp.shape, bf16),
            jax.ShapeDtypeStruct((8, width), f32),
            jax.ShapeDtypeStruct((8, 3 * width), f32),
        ]
        + [jax.ShapeDtypeStruct(s, f32) for s in shapes],
        in_specs=[pl.BlockSpec(memory_space=pltpu.SMEM), blk(width), blk(width), blk(width), blk(3 * width), blk(width), cube(PATCH_PAD, channels)]
        + [whole(w.shape) for w in (wp, wqkv, wout, params)]
        + [hbm] * len(grads),
        out_specs=[cube(PATCH_PAD, channels), cube(slots, width)] + [whole(s) for s in (wqkv.shape, wout.shape, wp.shape, (8, width), (8, 3 * width), *shapes)],
        scratch_shapes=[pltpu.VMEM(wqkv.shape, f32), pltpu.VMEM(wout.shape, f32), pltpu.VMEM(wp.shape, f32), pltpu.VMEM((n * rows, width), bf16), pltpu.VMEM((n * rows, 3 * width), bf16)]
        + (scatter_buffers(A, B, cuts, shapes) + scatter_sems(A, B, len(cuts)) if grads else []),
        compiler_params=pltpu.CompilerParams(vmem_limit_bytes=62 << 20, **remote),
        name="attend_back",
    )(lengths, dx2, x, h1, qkv, o, act, wp, wqkv, wout, params, *[split_rows(A, B, g) for g in grads])


class Total:
    def __init__(self, pc, j, send, recv, ssem, rsem):
        self.pc, self.send, self.recv = pc, send.at[j], recv.at[j]
        self.ssem, self.rsem = ssem.at[j], rsem.at[j]
        groups = [pc.bpeers, pc.dpeers]
        self.groups, at = [], 0
        for g in groups:
            self.groups.append([(at + k, dev) for k, dev in enumerate(g)])
            at += len(g)

    def copy(self, step, k, dev):
        return rcopy(self.send.at[step], self.recv.at[k], self.ssem.at[k], self.rsem.at[k], dev)

    def put(self, step, v):
        self.send[step] = v
        for k, dev in self.groups[step]:
            self.copy(step, k, dev).start()

    def take(self, step):
        v = self.send[step]
        for k, dev in self.groups[step]:
            self.copy(step, k, dev).wait_recv()
            v = v + self.recv[k]
        return v

    def begin(self, v):
        self.put(0, v)

    def middle(self):
        self.put(1, self.take(0))

    def end(self):
        return self.take(1)

    def drain(self):
        for step in range(2):
            for k, dev in self.groups[step]:
                self.copy(step, k, dev).wait_send()


def total_scratch(A, B, count, shape):
    peers = (B - 1) + (A - 1)
    return [pltpu.VMEM((count, 2) + shape, f32), pltpu.VMEM((count, peers) + shape, f32), DMA((count, peers)), DMA((count, peers))]


def tile_rows(rows):
    return -(-rows // 16) * 16


def together(rows):
    n = 1
    while n * rows % 16:
        n += 1
    return n


def unpack(src, dst, rows):
    padded, cols = src.shape[-2:]
    shards = dst.shape[0] // rows
    flat = src[...].reshape(shards * padded, cols)
    if padded == rows:
        dst[...] = flat
        return
    n = together(rows)
    pick = turn_rows((n * rows, n * padded), rows, padded)
    for t in range(shards // n):
        dst[t * n * rows : (t + 1) * n * rows] = dot(pick, flat[t * n * padded : (t + 1) * n * padded]).astype(bf16)


def turn_rows(shape, rows, padded):
    out, pos = iota(shape, 0), iota(shape, 1)
    shard = jnp.floor((out.astype(f32) + 0.5) * (1.0 / rows)).astype(jnp.int32)
    return jnp.where(pos == out + shard * (padded - rows), 1.0, 0.0).astype(bf16)


def pack(src, dst, rows):
    padded, cols = dst.shape[-2:]
    shards = src.shape[0] // rows
    if padded == rows:
        dst[...] = src.reshape(dst.shape)
        return
    n = together(rows)
    shape = (n * padded, n * rows)
    out, pos = iota(shape, 0), iota(shape, 1)
    shard = jnp.floor((out.astype(f32) + 0.5) * (1.0 / padded)).astype(jnp.int32)
    pick = jnp.where((pos == out - shard * (padded - rows)) & (out - shard * padded < rows), 1.0, 0.0).astype(bf16)
    parts = [dot(pick, src[t * n * rows : (t + 1) * n * rows]).astype(bf16) for t in range(shards // n)]
    dst[...] = jnp.concatenate(parts, 0).reshape(dst.shape)


def unpack_vectors(tab, out, sizes):
    shards = tab.shape[0] * tab.shape[1] * tab.shape[2] * tab.shape[3]
    flat = tab[...].reshape(shards, tab.shape[-2], tab.shape[-1])[:, 0, :]
    out[...] = jnp.zeros(out.shape, f32)
    for v, n in enumerate(sizes):
        wide = n * shards
        lane = iota((128, wide), 1)
        block = jnp.floor((lane.astype(f32) + 0.5) * (1.0 / n)).astype(jnp.int32)
        spot = jnp.where(iota((128, wide), 0) == lane - block * n, 1.0, 0.0).astype(bf16)
        rows = dot(flat[:, 128 * v : 128 * (v + 1)].astype(bf16), spot)
        owner = jnp.where(iota((shards, wide), 0) == block[:shards] if shards <= 128 else block, rows, 0.0)
        out[v : v + 1, :wide] = colsum(owner)


def make_taps(taps, grid):
    places = grid * grid
    i, j = iota((places, places), 0), iota((places, places), 1)
    col = i - grid * jnp.floor((i.astype(f32) + 0.5) * (1.0 / grid)).astype(jnp.int32)
    for t in range(9):
        dr, dc = t // 3 - 1, t % 3 - 1
        hit = (j == i + grid * dr + dc) & (col + dc >= 0) & (col + dc < grid)
        taps[t] = jnp.where(hit, 1.0, 0.0).astype(bf16)


def rows_of(vectors):
    rows = []
    for v in vectors:
        rows += [v[:, q : q + 256] for q in range(0, v.shape[1], 256)]
    if len(rows) < 8:
        rows.append(jnp.zeros((8 - len(rows), 256), f32))
    return jnp.concatenate(rows, 0)


def vectors_of(block, width):
    per = width // 256
    take = lambda k: jnp.concatenate([block[k * per + q : k * per + q + 1] for q in range(per)], 1)
    return take(0), take(1)


VECTORS = ("bn1_gain", "bn1_bias", "bn2_gain", "bn2_bias", "bn3_gain", "bn3_bias", "b_patch", "ln1_gain", "ln1_bias", "b_q", "b_v", "b_out", "ln2_gain", "ln2_bias", "b_up", "b_down")


def moments(s1, s2, total_rows, gain, bias):
    mean = s1 / total_rows
    inv = lax.rsqrt(s2 / total_rows - mean * mean + bn_eps)
    return mean, inv


def stem_kernel(A, B, items, n_mats, sizes, shard_rows, total_rows, *refs):
    n_vec = len(sizes)
    feats, vecs, refs = refs[0], refs[1 : 1 + n_vec], refs[1 + n_vec :]
    near, far_in, refs = refs[:3], refs[3 : n_mats - 1], refs[n_mats - 1 :]
    n_far = n_mats - 4
    far, refs = refs[:n_far], refs[n_far:]
    (act_h, r_h, c_h, e_h, params, stats, w_red, w_conv, w_exp), refs = refs[:9], refs[9:]
    (act, r_o, c_o, e_o, out_sems), refs = refs[:5], refs[5:]
    (p_red, tab, p_conv, p_exp, taps, cols), refs = refs[:6], refs[6:]
    mine, refs = refs[:4], refs[4:]
    sums, sems = refs[:4], refs[4:]
    pc = Place(A, B)
    for src, dst in zip(near, (mine[0], mine[2], mine[3])):
        dst[...] = dot(jnp.where(iota((dst.shape[0], src.shape[0]), 0) == iota((dst.shape[0], src.shape[0]), 1), 1.0, 0.0).astype(bf16), src[...]).astype(bf16)
    mine[1][...] = jnp.zeros(mine[1].shape, f32)
    for v, ref in enumerate(vecs):
        mine[1][:, 128 * v : 128 * v + sizes[v]] = ref[...].astype(f32)
    shards = [*mine, *far_in]
    pc.greet()
    dsts = [p_red, tab, p_conv, p_exp, *far]
    moves = [GatherItem(pc, j, c, order, shards[i], dsts[i], sems) for j, (i, c, order) in enumerate(items)]
    adds = [Total(pc, j, *sums) for j in range(3)]
    examples, patches, channels = feats.shape
    grid = GRID
    vec = lambda v, width: params[v : v + 1, :width]

    def each(fn, width):
        zero = jnp.zeros((1, width), f32)

        def body(i, s):
            v = fn(i)
            return s[0] + colsum(v), s[1] + colsum(v * v)

        return lax.fori_loop(0, examples, body, (zero, zero))

    def norm(v, j, width):
        return (v - stats[2 * j : 2 * j + 1, :width]) * stats[2 * j + 1 : 2 * j + 2, :width] * vec(2 * j, width) + vec(2 * j + 1, width)

    def keep(j, width):
        s1, s2 = vectors_of(adds[j].end(), width)
        mean, inv = moments(s1, s2, total_rows, None, None)
        stats[2 * j : 2 * j + 1, :width] = mean
        stats[2 * j + 1 : 2 * j + 2, :width] = inv

    narrow = r_o.shape[2]

    def first():
        moves[0].arrived()
        unpack(p_red, w_red, shard_rows[0])

        def one(i):
            v = dot(feats[i], w_red[...])
            r_o[i] = v
            return v

        adds[0].begin(rows_of(each(one, narrow)))

    def vectors():
        moves[1].arrived()
        unpack_vectors(tab, params, sizes)

    def second():
        keep(0, narrow)

        def one(i):
            ra = smooth(norm(r_o[i], 0, narrow)).astype(bf16)
            for t in range(9):
                cols[:, t * narrow : (t + 1) * narrow] = dot(taps[t], ra).astype(bf16)
            v = dot(cols[...], w_conv[...])
            c_o[i] = v
            return v

        adds[1].begin(rows_of(each(one, narrow)))

    def third():
        keep(1, narrow)

        def one(i):
            ca = smooth(norm(c_o[i], 1, narrow)).astype(bf16)
            v = dot(ca, w_exp[...])
            e_o[i] = v
            return v

        adds[2].begin(rows_of(each(one, channels)))

    def act_copy(i):
        return pltpu.make_async_copy(act.at[i], act_h.at[i], out_sems.at[3 + i])

    def fourth():
        keep(2, channels)
        wide = spread(act.shape[1], patches, patches)

        def body(i, _):
            v = norm(e_o[i], 2, channels) + feats[i].astype(f32)
            act[i] = dot(wide, smooth(v).astype(bf16)).astype(bf16)
            act_copy(i).start()
            return 0

        lax.fori_loop(0, examples, body, 0)

    saved = [pltpu.make_async_copy(v, h, out_sems.at[k]) for k, (v, h) in enumerate(((r_o, r_h), (c_o, c_h), (e_o, e_h)))]
    make_taps(taps, grid)
    stats[...] = jnp.zeros(stats.shape, f32)

    def ready_conv():
        moves[2].arrived()
        unpack(p_conv, w_conv, shard_rows[1])
        vectors()

    def ready_exp():
        moves[3].arrived()
        unpack(p_exp, w_exp, shard_rows[2])

    hooks = {8: [first], 10: [adds[0].middle, saved[0].start, ready_conv], 12: [second], 14: [adds[1].middle, saved[1].start, ready_exp], 16: [third], 18: [adds[2].middle, saved[2].start], 20: [fourth]}
    wave(moves, (0, 2, 4, 6), ["start", "second", "third", "fourth"], hooks)
    for m in moves:
        m.arrived()
    for m in moves:
        m.drain()
    for t in adds:
        t.drain()
    for t in saved:
        t.wait()
    lax.fori_loop(0, examples, lambda i, _: (act_copy(i).wait(), 0)[1], 0)


def stem_forward(A, B, feats, vecs, mats, pad_rows, parts, cid):
    A2, Z, count = A // 2, B // 2, A * B
    examples, patches, channels = feats.shape
    near, far = mats[:3], mats[3:]
    sizes = [v.shape[0] for v in vecs]
    shard_rows = [m.shape[0] for m in near]
    pads = [jax.ShapeDtypeStruct((tile_rows(m.shape[0]), m.shape[1]), bf16) for m in near]
    shards = [pads[0], jax.ShapeDtypeStruct((1, 128 * len(vecs)), f32), pads[1], pads[2], *far]
    items = cut([(s.shape[1], q) for s, q in zip(shards, (1, 1, 1, 1) + parts)])
    shape = lambda s: (A2, 2, Z, 2) + s.shape
    narrow = near[0].shape[1]
    hbm, vm = pl.BlockSpec(memory_space=pl.ANY), pl.BlockSpec(memory_space=pltpu.VMEM)
    full = [(m.shape[0] * count, m.shape[1]) for m in near]
    outs = pl.pallas_call(
        functools.partial(stem_kernel, A, B, items, len(shards), sizes, shard_rows, float(examples * count * patches)),
        out_shape=[jax.ShapeDtypeStruct(shape(s), s.dtype) for s in far]
        + [
            jax.ShapeDtypeStruct((examples, pad_rows, channels), bf16),
            jax.ShapeDtypeStruct((examples, patches, narrow), f32),
            jax.ShapeDtypeStruct((examples, patches, narrow), f32),
            jax.ShapeDtypeStruct((examples, patches, channels), f32),
            jax.ShapeDtypeStruct((16, sizes[13] * count), f32),
            jax.ShapeDtypeStruct((8, channels), f32),
        ]
        + [jax.ShapeDtypeStruct(s, bf16) for s in full],
        in_specs=[vm] * (1 + len(vecs) + 3) + [hbm] * len(far),
        out_specs=[hbm] * (len(far) + 4) + [vm] * 5,
        scratch_shapes=[
            pltpu.VMEM((examples, pad_rows, channels), bf16),
            pltpu.VMEM((examples, patches, narrow), f32),
            pltpu.VMEM((examples, patches, narrow), f32),
            pltpu.VMEM((examples, patches, channels), f32),
            DMA((3 + examples,)),
        ]
        + [pltpu.VMEM(shape(s), s.dtype) for s in shards[:4]]
        + [pltpu.VMEM((9, patches, patches), bf16), pltpu.VMEM((patches, full[1][0]), bf16)]
        + [pltpu.VMEM(s.shape, s.dtype) for s in shards[:4]]
        + total_scratch(A, B, 3, (8, 256))
        + gather_sems(A, B, len(items)),
        compiler_params=pltpu.CompilerParams(collective_id=cid, has_side_effects=True, vmem_limit_bytes=60 << 20),
        name="stem",
    )(feats, *[v[None] for v in vecs], *near, *far)
    return [g.reshape(-1, g.shape[-1]) for g in outs[: len(far)]], outs[len(far) :]


class Run:
    pass


class Written:
    def __init__(self, out):
        self.out = out

    def second(self):
        pass

    third = fourth = arrived = second


def stem_back_kernel(A, B, cuts, near_rows, total_rows, sizes, n_far, inside, *refs):
    (dact_h, feats_h, red_h, conv_h, expand_h, params, stats, w_red, w_conv, w_exp, small_f, small_b, small_a, small_q), refs = refs[:14], refs[14:]
    far, refs = refs[:n_far], refs[n_far:]
    (gfeats_h, shares), refs = refs[:2], refs[2:]
    far_out, near_out, refs = refs[:n_far], refs[n_far : n_far + 3], refs[n_far + 3 :]
    (dact, feats, expand, red, conv, gfeats, ex_sems, in_sems), refs = refs[:8], refs[8:]
    (ds_s, dy_s, ca_s, taps, gred, gconv, gexp, k_red, k_conv, k_exp), refs = refs[:10], refs[10:]
    sums, vsum, refs = refs[:4], refs[4:8], refs[8:]
    bufs, sems = refs[: 5 * len(cuts)], refs[5 * len(cuts) :]
    def load(k, i):
        src, dst = ((dact_h, dact), (feats_h, feats), (expand_h, expand))[k]
        return pltpu.make_async_copy(src.at[i], dst.at[i], ex_sems.at[k, i])

    def leave_feats(i):
        return pltpu.make_async_copy(gfeats.at[i], gfeats_h.at[i], ex_sems.at[3, i])

    load_conv, load_red = (pltpu.make_async_copy(a, b, in_sems.at[k]) for k, (a, b) in enumerate(((conv_h, conv), (red_h, red))))
    for i in range(feats.shape[0]):
        for k in range(3):
            load(k, i).start()
    load_conv.start()
    load_red.start()
    pc = Place(A, B)
    pc.greet()
    moves = scatter_items(pc, cuts, [*far, k_exp, k_conv, k_red], [*far_out, near_out[2], near_out[1], near_out[0]], bufs, sems)
    big, late = (moves[:-3], moves[-3:]) if inside else (moves, [Written(o) for o in (near_out[2], near_out[1], near_out[0])])
    m_exp, m_conv, m_red = late

    def leave(move, grad, packed, rows):
        if inside:
            pack(grad[...].astype(bf16), packed, rows)
            move.start()
        else:
            move.out[...] = grad[...].astype(bf16)

    adds = [Total(pc, j, *sums) for j in range(3)]
    vec_sum = Total(pc, 0, *vsum)
    examples, patches, channels = feats.shape
    narrow, width = red.shape[2], small_a.shape[1]
    for m in big:
        m.start()
    rows = [small_a[3:4], small_a[0:1], small_a[1:2], small_q[0:1, :width], small_q[0:1, 2 * width :], small_a[2:3], small_f[1:2], small_f[2:3]]
    rows += [small_b[:, q : q + width] for q in range(0, small_b.shape[1], width)]
    rows += [small_f[0:1]]
    vec_sum.begin(jnp.concatenate(rows + [jnp.zeros((16 - len(rows), width), f32)], 0))
    make_taps(taps, GRID)

    def hat_of(ref, i, j, w):
        return (ref[i] - stats[2 * j : 2 * j + 1, :w]) * stats[2 * j + 1 : 2 * j + 2, :w]

    def point(hat, j, w):
        return hat * params[2 * j : 2 * j + 1, :w] + params[2 * j + 1 : 2 * j + 2, :w]

    def each(fn, w):
        zero = jnp.zeros((1, w), f32)

        def body(i, s):
            dy, hat = fn(i)
            return s[0] + colsum(dy), s[1] + colsum(dy * hat)

        return lax.fori_loop(0, examples, body, (zero, zero))

    def norm_back(dy, hat, j, w, totals):
        scale = stats[2 * j + 1 : 2 * j + 2, :w] * params[2 * j : 2 * j + 1, :w]
        return (scale * (dy - totals[0] * (1.0 / total_rows) - hat * (totals[1] * (1.0 / total_rows)))).astype(bf16)

    run = Run()

    def fifth():
        def one(i):
            for k in range(3):
                load(k, i).wait()
            hat = hat_of(expand, i, 2, channels)
            _, slope = smooth_both(point(hat, 2, channels) + feats[i].astype(f32))
            dy = dact[i, :patches] * slope
            ds_s[i] = dy
            return dy, hat

        adds[2].begin(rows_of(each(one, channels)))

    def sixth():
        load_conv.wait()
        run.t3 = vectors_of(adds[2].end(), channels)
        gexp[...] = jnp.zeros(gexp.shape, f32)

        def one(i):
            de = norm_back(ds_s[i], hat_of(expand, i, 2, channels), 2, channels, run.t3)
            hat = hat_of(conv, i, 1, narrow)
            ca, slope = smooth_both(point(hat, 1, narrow))
            gexp[...] += dot_tn(ca.astype(bf16), de)
            dy = dot_nt(de, w_exp[...]) * slope
            dy_s[i] = dy
            return dy, hat

        adds[1].begin(rows_of(each(one, narrow)))
        leave(m_exp, gexp, k_exp, near_rows[2])

    def seventh():
        load_red.wait()
        run.t2 = vectors_of(adds[1].end(), narrow)
        gconv[...] = jnp.zeros(gconv.shape, f32)

        def one(i):
            dc = norm_back(dy_s[i], hat_of(conv, i, 1, narrow), 1, narrow, run.t2)
            hat = hat_of(red, i, 0, narrow)
            ra, slope = smooth_both(point(hat, 0, narrow))
            turned = ra.T.astype(bf16)
            dra = jnp.zeros((patches, narrow), f32)
            for t in range(9):
                moved = dot(taps[8 - t], dc).astype(bf16)
                at = slice(t * narrow, (t + 1) * narrow)
                gconv[at] += dot(turned, moved)
                dra = dra + dot_nt(moved, w_conv[at])
            dy = dra * slope
            dy_s[i] = dy
            return dy, hat

        adds[0].begin(rows_of(each(one, narrow)))
        leave(m_conv, gconv, k_conv, near_rows[1])

    def eighth():
        run.t1 = vectors_of(adds[0].end(), narrow)
        gred[...] = jnp.zeros(gred.shape, f32)

        def body(i, _):
            dr = norm_back(dy_s[i], hat_of(red, i, 0, narrow), 0, narrow, run.t1)
            ca_s[i] = dr
            gred[...] += dot_tn(feats[i], dr)
            return 0

        lax.fori_loop(0, examples, body, 0)
        leave(m_red, gred, k_red, near_rows[0])

    def ninth(lo, hi):
        def body(i, _):
            gfeats[i] = (ds_s[i] + dot_nt(ca_s[i], w_red[...])).astype(bf16)
            leave_feats(i).start()
            return 0

        lax.fori_loop(lo, hi, body, 0)

    def finish():
        v = vec_sum.end()
        me = pc.a * B + pc.b
        one = lambda k: v[k : k + 1]
        rows = [run.t1[1], run.t1[0], run.t2[1], run.t2[0], run.t3[1], run.t3[0], one(0), one(1), one(2), jnp.concatenate([one(3), one(4)], 1)]
        rows += [one(5), one(6), one(7), jnp.concatenate([one(k) for k in range(8, 8 + small_b.shape[1] // width)], 1), one(8 + small_b.shape[1] // width)]
        for k, row in enumerate(rows):
            wide = row.shape[1]
            turn = lax.rem(wide - me * sizes[k], wide)
            shares[k : k + 1] = pltpu.roll(jnp.broadcast_to(row, (8, wide)), turn, 1)[0:1, :128]
        shares[15:16] = jnp.zeros((1, 128), f32)

    queue = wave_stages(big, (0, 2, 4, 6), ["second", "third", "fourth", "arrived"])

    def advance(count):
        for _ in range(min(count, len(queue))):
            queue.pop(0)()

    fifth()
    advance(2)
    adds[2].middle()
    vec_sum.middle()
    advance(4)
    sixth()
    advance(2)
    adds[1].middle()
    m_exp.second()
    advance(4)
    seventh()
    m_exp.third()
    advance(2)
    adds[0].middle()
    m_conv.second()
    m_exp.fourth()
    advance(4)
    eighth()
    m_conv.third()
    advance(2)
    m_red.second()
    ninth(0, examples // 2)
    m_conv.fourth()
    m_red.third()
    advance(2)
    ninth(examples // 2, examples)
    m_red.fourth()
    finish()
    advance(len(queue))
    m_exp.arrived()
    m_conv.arrived()
    m_red.arrived()
    for m in moves:
        m.drain()
    for s in adds + [vec_sum]:
        s.drain()
    lax.fori_loop(0, examples, lambda i, _: (leave_feats(i).wait(), 0)[1], 0)


def stem_backward(A, B, dact, feats, red, conv, expand, params, stats, w_red, w_conv, w_exp, smalls, sizes, grads, parts, inside, cid):
    A2, Z, count = A // 2, B // 2, A * B
    examples, patches, channels = feats.shape
    narrow = red.shape[2]
    near = [w_red, w_conv, w_exp]
    near_rows = [w.shape[0] // count for w in near]
    packed = [(tile_rows(r), w.shape[1]) for r, w in zip(near_rows, near)]
    cuts = cut([(g.shape[1], q) for g, q in zip(grads, parts)] + [(p[1], 1) for p in reversed(packed) if inside])
    shapes = [(g.shape[0] // count, g.shape[1]) for g in grads] + packed[::-1]
    outs = [jax.ShapeDtypeStruct(feats.shape, bf16), jax.ShapeDtypeStruct((16, 128), f32)]
    outs += [jax.ShapeDtypeStruct(s, f32) for s in shapes[: len(grads)]]
    outs += [jax.ShapeDtypeStruct((r, w.shape[1]), f32) if inside else jax.ShapeDtypeStruct(w.shape, bf16) for r, w in zip(near_rows, near)]
    hbm, vm = pl.BlockSpec(memory_space=pl.ANY), pl.BlockSpec(memory_space=pltpu.VMEM)
    lead = (A2, 2, Z, 2)
    return pl.pallas_call(
        functools.partial(stem_back_kernel, A, B, cuts, near_rows, float(examples * count * patches), sizes, len(grads), inside),
        out_shape=outs,
        in_specs=[hbm] * 5 + [vm] * 9 + [hbm] * len(grads),
        out_specs=[hbm] + [vm] * (len(outs) - 1),
        scratch_shapes=[pltpu.VMEM(a.shape, a.dtype) for a in (dact, feats, expand, red, conv, feats)]
        + [
            DMA((4, examples)),
            DMA((2,)),
            pltpu.VMEM((examples, patches, channels), f32),
            pltpu.VMEM((examples, patches, narrow), f32),
            pltpu.VMEM((examples, patches, narrow), bf16),
            pltpu.VMEM((9, patches, patches), bf16),
        ]
        + [pltpu.VMEM(w.shape, f32) for w in near]
        + [pltpu.VMEM(lead + p if inside else (16, 128), bf16) for p in packed]
        + total_scratch(A, B, 3, (8, 256))
        + total_scratch(A, B, 1, (16, smalls[2].shape[1]))
        + (scatter_buffers(A, B, cuts, shapes) + scatter_sems(A, B, len(cuts)) if cuts else []),
        compiler_params=pltpu.CompilerParams(collective_id=cid, has_side_effects=True, vmem_limit_bytes=62 << 20),
        name="stem_back",
    )(dact, feats, red, conv, expand, params, stats, w_red, w_conv, w_exp, *smalls, *[split_rows(A, B, g) for g in grads])


def finish_kernel(n, *refs):
    shares, ins, outs, vecs = refs[0], refs[1 : 1 + n], refs[1 + n : 1 + 2 * n], refs[1 + 2 * n :]
    for a, b in zip(ins, outs):
        b[...] = a[...]
    for v, ref in enumerate(vecs):
        ref[...] = shares[v, : ref.shape[0]]


def finish(shares, sizes, arrays):
    vm = pl.BlockSpec(memory_space=pltpu.VMEM)
    n = len(arrays)
    outs = pl.pallas_call(
        functools.partial(finish_kernel, n),
        out_shape=[jax.ShapeDtypeStruct(a.shape, a.dtype) for a in arrays] + [jax.ShapeDtypeStruct((s,), f32) for s in sizes],
        in_specs=[vm] * (1 + n),
        out_specs=[vm] * (n + len(sizes)),
        compiler_params=pltpu.CompilerParams(vmem_limit_bytes=48 << 20),
        name="finish",
    )(shares, *arrays)
    return outs[:n], outs[n:]


AXES = ("dp", "fsdp")


def local(
    feats, text, lengths, cotangent,
    w_red, bn1_gain, bn1_bias, w_conv, bn2_gain, bn2_bias, w_exp, bn3_gain, bn3_bias, w_patch, b_patch,
    ln1_gain, ln1_bias, w_qkv, b_qv, w_out, b_out, ln2_gain, ln2_bias, w_up, b_up, w_down, b_down,
):
    A, B = lax.axis_size("dp"), lax.axis_size("fsdp")
    vecs = (bn1_gain, bn1_bias, bn2_gain, bn2_bias, bn3_gain, bn3_bias, b_patch, ln1_gain, ln1_bias, b_qv, b_out, ln2_gain, ln2_bias, b_up, b_down)
    sizes = [v.shape[0] for v in vecs]
    patches, slots = feats.shape[1], text.shape[1]
    far, near = stem_forward(A, B, feats, vecs, (w_red, w_conv, w_exp, w_patch, w_qkv, w_out, w_up, w_down), PATCH_PAD, (1, 3, 1, 4, 3), 0)
    full_patch, full_qkv, full_out, full_up, full_down = far
    act, red, conv, expand, params, stats, full_red, full_conv, full_exp = near
    x, h1, qkv, o, x2, h2 = attend(lengths, act, text, full_patch, full_qkv, full_out, params, patches, 2)
    output, dx2, g_up, g_down, small_b, small_f = ffn(lengths, h2, x2, cotangent, full_up, full_down, params, patches, 2, 512)
    inside = w_qkv.shape[0] >= 16
    first = [g_up, g_down] if inside else []
    dact, grad_text, g_qkv, g_out, g_patch, small_a, small_q, *sums = attend_back(
        A, B, lengths, dx2, x, h1, qkv, o, act, full_patch, full_qkv, full_out, params, first, (4, 3)[: len(first)], slots, patches, 1, 1
    )
    second = [g_qkv, g_out, g_patch] if inside else []
    grad_feats, shares, *more = stem_backward(
        A, B, dact, feats, red, conv, expand, params, stats, full_red, full_conv, full_exp, (small_f, small_b, small_a, small_q), sizes, second, (3, 1, 1)[: len(second)], inside, 2
    )
    if not inside:
        sums = [lax.psum_scatter(g.astype(f32), AXES, scatter_dimension=0, tiled=True) for g in (g_up, g_down)]
        more = [lax.psum_scatter(g.astype(f32), AXES, scatter_dimension=0, tiled=True) for g in (g_qkv, g_out, g_patch, *more)]
    (grad_feats, s_up, s_down, s_qkv, s_out, s_patch, s_red, s_conv, s_exp), vectors = finish(shares, sizes, [grad_feats, *sums, *more])
    (s_bn1_gain, s_bn1_bias, s_bn2_gain, s_bn2_bias, s_bn3_gain, s_bn3_bias, s_b_patch, s_ln1_gain, s_ln1_bias, s_b_qv, s_b_out, s_ln2_gain, s_ln2_bias, s_b_up, s_b_down) = vectors
    return (
        output, grad_feats, grad_text,
        s_red, s_bn1_gain, s_bn1_bias, s_conv, s_bn2_gain, s_bn2_bias, s_exp, s_bn3_gain, s_bn3_bias, s_patch, s_b_patch,
        s_ln1_gain, s_ln1_bias, s_qkv, s_b_qv, s_out, s_b_out, s_ln2_gain, s_ln2_bias, s_up, s_b_up, s_down, s_b_down,
    )


def solution(mesh):
    every = ("dp", "fsdp")
    v, m, t = P(every), P(every, None), P(every, None, None)
    weights = (m, v, v, m, v, v, m, v, v, m, v, v, v, m, v, m, v, v, v, m, v, m, v)
    return jax.shard_map(local, mesh=mesh, in_specs=(t, t, v, t) + weights, out_specs=(t, t, t) + weights, check_vma=False)
```

time: 1000 us -> 397 us (0.40)
  matrix products: 286 us -> 0 us
  local copies, waits for them, and re-layouts: 242 us -> 8.34 us
  other arithmetic: 135 us -> 0 us
  Pallas kernels: 319 us -> 382 us
    dot_general x30 -> x0, matrix products: 286 us -> none  [the longest x8 80.4 us: right_product(): lax.dot_general(left, right, (((1,), (1,)), ((), ())), preferred_element_...]
    reshape x13 -> x0, local copies, waits for them, and re-layouts: 80.2 us -> none  [the longest x1 22.4 us: forward_pass(): qkv = qkv.reshape(examples, seq_len, 3, head_count, HEAD_DIM)]
    pallas_call x9 -> x6, Pallas kernels: 319 us -> 382 us  [the longest x1 103 us: stem_forward(): pl.pallas_call(functools.partial(stem_kernel, A, B, items, len(shards), s...]
    convert_element_type x24 -> x0, other arithmetic: 47 us -> none  [the longest x1 24.4 us: local(): (probs * (g_probs - jnp.sum(probs * g_probs, -1, keepdims=True))).astype(...]
    sub x1 -> x0, other arithmetic: 37.4 us -> none  [forward_pass(): expo_scores = jnp.exp(scores - top_score)]
    convert_element_type x23 -> x0, local copies, waits for them, and re-layouts: 36.2 us -> none  [the longest x1 19.5 us: local(): jnp.stack([g_query, g_key, g_value], 2).astype(jnp.bfloat16)]
    unnamed x249 -> x23, local copies, waits for them, and re-layouts: 44.2 us -> 8.34 us
    reduce_sum x10 -> x0, other arithmetic: 32 us -> none  [the longest x3 10.2 us: normed(): center = values - jnp.mean(values, -1, keepdims=True)]
where the time goes in v2:
time: 397 us; the launch traced here: 391 us
  Pallas kernels  382 us (96%)
  local copies, waits for them, and re-layouts  8.34 us (2%)
    pallas_call x1, Pallas kernels, stem_forward(): pl.pallas_call(functools.partial(stem_kernel, A, B, items, len(shards), s...  103 us
    pallas_call x1, Pallas kernels, attend_back(): pl.pallas_call(functools.partial(attend_back_kernel, A, B, n, patches, sl...  94.5 us
    pallas_call x1, Pallas kernels, stem_backward(): pl.pallas_call(functools.partial(stem_back_kernel, A, B, cuts, near_rows,...  79.4 us
    pallas_call x1, Pallas kernels, ffn(): pl.pallas_call(functools.partial(ffn_kernel, n, patches), grid=(hidden //...  67.4 us
    pallas_call x1, Pallas kernels, attend(): pl.pallas_call(functools.partial(attend_kernel, n, patches), grid=(steps,...  35.5 us
    unnamed x23, local copies, waits for them, and re-layouts  8.34 us

profile of v2, /device:TPU:0, one launch (start us, length us, event | category | flops | bytes accessed | tf_op | source)
XLA Modules:
  0.0 391.5 jit_solution(12418159021763162034)
XLA Ops:
  0.7 103.2 %stem.1 = (bf16[2,2,4,2,32,768]{5,4,3,2,1,0:T(8,128)(2,1)}, bf16[2,2,4,2,24,2304]{5,4,3,2,1,0:T(8,128)(2,1)}, bf16[2,2,4,2,24,768]{5,4,3,2,1,0:T(8,128)(2,1)}, b...) custom-call(bf16[6,196,1024]{2,1,0:T(8,128)(2,1)} %refs_1_.1, ...), custom_call_target="tpu_custom_call" | custom-call | tf_op jit(solution)/shard_map/stem/pallas_call | solution.py:939
  103.9 35.5 %attend.1 = (f32[1632,768]{1,0:T(8,128)}, bf16[1632,768]{1,0:T(8,128)(2,1)}, bf16[1632,2304]{1,0:T(8,128)(2,1)}, bf16[1632,768]{1,0:T(8,128)(2,1)}, f32[1632,768]{1,0:T(8,128)}, /*index=5*/bf16[1632,768]{1,0:T(8,128)(2,1)}) custom-call(s32[6]{0:T(128)} %refs_0_.3, bf16[6,208,1024]{2,1,0:T(8,128)(2,1)} %get-tuple-element.93.act.refs_6_, ...), custom_call_target="tpu_custom_call" | custom-call | tf_op jit(solution)/shard_map/attend/pallas_call | solution.py:429
  139.4 67.4 %ffn.1 = (bf16[6,260,768]{2,1,0:T(8,128)(2,1)}, f32[1632,768]{1,0:T(8,128)}, bf16[768,3072]{1,0:T(8,128)(2,1)}, bf16[3072,768]{1,0:T(8,128)(2,1)}, f32[1,3072]{1,0:T(1,128)}, /*index=5*/f32[8,768]{1,0:T(8,128)}) custom-call(s32[6]{0:T(128)} %refs_0_.3, bf16[1632,768]{1,0:T(8,128)(2,1)} %get-tuple-element.98.h2, f32[1632,768]{1,0:T(8,128)} %get-tuple-element.99.x2_h, ...), custom_call_target="tpu_custom_call" | custom-call | tf_op jit(solution)/shard_map/ffn/pallas_call | solution.py:522
  206.8 94.5 %attend_back.1 = (f32[6,208,1024]{2,1,0:T(8,128)}, bf16[6,64,768]{2,1,0:T(8,128)(2,1)}, bf16[768,2304]{1,0:T(8,128)(2,1)}, bf16[768,768]{1,0:T(8,128)(2,1)}, bf1...) custom-call(s32[6]{0:T(128)} %refs_0_.3, ...), custom_call_target="tpu_custom_call" | custom-call | tf_op jit(solution)/shard_map/attend_back/pallas_call | solution.py:638
  301.3 0.0 copy-start.1
  301.4 0.0 copy-start.2
  301.4 0.0 copy-start.10
  301.4 79.4 %stem_back.1 = (bf16[6,196,1024]{2,1,0:T(8,128)(2,1)}, f32[16,128]{1,0:T(8,128)}, f32[24,2304]{1,0:T(8,128)}, f32[24,768]{1,0:T(8,128)}, f32[32,768]{1,0:T(8,128...) custom-call(f32[6,208,1024]{2,1,0:T(8,128)} %get-tuple-element.110.refs_0_, ...), custom_call_target="tpu_custom_call" | custom-call | tf_op jit(solution)/shard_map/stem_back/pallas_call | solution.py:1197
  380.8 0.0 copy-done.1
  380.8 0.0 copy-done.2
  380.8 0.0 copy-start
  380.8 1.7 copy-done
  382.5 0.0 copy-start.3
  382.5 0.9 copy-done.3
  383.5 0.0 copy-start.4
  383.5 0.9 copy-done.4
  384.4 0.0 copy-start.5
  384.4 0.9 copy-done.5
  385.2 0.0 copy-start.6
  385.2 0.9 copy-done.6
  386.1 0.0 copy-start.7
  386.1 0.8 copy-done.7
  386.9 0.0 copy-start.8
  386.9 0.8 copy-done.8
  387.6 0.0 copy-start.9
  387.6 0.7 copy-done.9
  388.4 2.0 finish.1
  390.4 0.0 copy-done.10
  390.4 0.8 copy.54
Async XLA Ops:
  301.3 79.5 %copy-start.1 = (f32[24,3072]{1,0:T(8,128)S(1)}, f32[24,3072]{1,0:T(8,128)}, u32[]{:S(2)}) copy-start(f32[24,3072]{1,0:T(8,128)} %get-tuple-element.127.refs_2_) | copy-start | bytes 884740
  301.4 79.5 %copy-start.2 = (f32[96,768]{1,0:T(8,128)S(1)}, f32[96,768]{1,0:T(8,128)}, u32[]{:S(2)}) copy-start(f32[96,768]{1,0:T(8,128)} %get-tuple-element.128.refs_3_) | copy-start | bytes 884740
  301.4 89.0 %copy-start.10 = (bf16[6,64,768]{2,1,0:T(8,128)(2,1)S(1)}, bf16[6,64,768]{2,1,0:T(8,128)(2,1)}, u32[]{:S(2)}) copy-start(bf16[6,64,768]{2,1,0:T(8,128)(2,1)} %get-tuple-element.188) | copy-start | bytes 1769476
  380.8 1.7 copy-start
  382.5 0.9 copy-start.3
  383.5 0.9 copy-start.4
  384.4 0.9 copy-start.5
  385.2 0.9 copy-start.6
  386.1 0.8 copy-start.7
  386.9 0.8 copy-start.8
  387.6 0.7 copy-start.9

commit v3 on v2

--- a/solution.py
+++ b/solution.py
@@ -830,7 +830,7 @@
             v = fn(i)
             return s[0] + colsum(v), s[1] + colsum(v * v)
 
-        return lax.fori_loop(0, examples, body, (zero, zero))
+        return lax.fori_loop(0, examples, body, (zero, zero), unroll=3)
 
     def norm(v, j, width):
         return (v - stats[2 * j : 2 * j + 1, :width]) * stats[2 * j + 1 : 2 * j + 2, :width] * vec(2 * j, width) + vec(2 * j + 1, width)
@@ -895,7 +895,7 @@
             act_copy(i).start()
             return 0
 
-        lax.fori_loop(0, examples, body, 0)
+        lax.fori_loop(0, examples, body, 0, unroll=3)
 
     saved = [pltpu.make_async_copy(v, h, out_sems.at[k]) for k, (v, h) in enumerate(((r_o, r_h), (c_o, c_h), (e_o, e_h)))]
     make_taps(taps, grid)
@@ -1042,7 +1042,7 @@
             dy, hat = fn(i)
             return s[0] + colsum(dy), s[1] + colsum(dy * hat)
 
-        return lax.fori_loop(0, examples, body, (zero, zero))
+        return lax.fori_loop(0, examples, body, (zero, zero), unroll=3)
 
     def norm_back(dy, hat, j, w, totals):
         scale = stats[2 * j + 1 : 2 * j + 2, :w] * params[2 * j : 2 * j + 1, :w]
@@ -1219,22 +1219,31 @@
 
 
 def finish_kernel(n, *refs):
-    shares, ins, outs, vecs = refs[0], refs[1 : 1 + n], refs[1 + n : 1 + 2 * n], refs[1 + 2 * n :]
-    for a, b in zip(ins, outs):
-        b[...] = a[...]
+    shares, ins, outs, refs = refs[0], refs[1 : 1 + n], refs[1 + n : 1 + 2 * n], refs[1 + 2 * n :]
+    vecs, bufs, sems = refs[: -n - 1], refs[-n - 1 : -1], refs[-1]
+    loads = [pltpu.make_async_copy(a, b, sems.at[0, k]) for k, (a, b) in enumerate(zip(ins, bufs))]
+    stores = [pltpu.make_async_copy(a, b, sems.at[1, k]) for k, (a, b) in enumerate(zip(bufs, outs))]
+    for c in loads:
+        c.start()
     for v, ref in enumerate(vecs):
         ref[...] = shares[v, : ref.shape[0]]
+    for load, store in zip(loads, stores):
+        load.wait()
+        store.start()
+    for c in stores:
+        c.wait()
 
 
 def finish(shares, sizes, arrays):
-    vm = pl.BlockSpec(memory_space=pltpu.VMEM)
+    hbm, vm = pl.BlockSpec(memory_space=pl.ANY), pl.BlockSpec(memory_space=pltpu.VMEM)
     n = len(arrays)
     outs = pl.pallas_call(
         functools.partial(finish_kernel, n),
         out_shape=[jax.ShapeDtypeStruct(a.shape, a.dtype) for a in arrays] + [jax.ShapeDtypeStruct((s,), f32) for s in sizes],
-        in_specs=[vm] * (1 + n),
-        out_specs=[vm] * (n + len(sizes)),
-        compiler_params=pltpu.CompilerParams(vmem_limit_bytes=48 << 20),
+        in_specs=[vm] + [hbm] * n,
+        out_specs=[hbm] * n + [vm] * len(sizes),
+        scratch_shapes=[pltpu.VMEM(a.shape, a.dtype) for a in arrays] + [DMA((2, n))],
+        compiler_params=pltpu.CompilerParams(vmem_limit_bytes=60 << 20),
         name="finish",
     )(shares, *arrays)
     return outs[:n], outs[n:]
@@ -1269,7 +1278,7 @@
     if not inside:
         sums = [lax.psum_scatter(g.astype(f32), AXES, scatter_dimension=0, tiled=True) for g in (g_up, g_down)]
         more = [lax.psum_scatter(g.astype(f32), AXES, scatter_dimension=0, tiled=True) for g in (g_qkv, g_out, g_patch, *more)]
-    (grad_feats, s_up, s_down, s_qkv, s_out, s_patch, s_red, s_conv, s_exp), vectors = finish(shares, sizes, [grad_feats, *sums, *more])
+    (grad_feats, grad_text, s_up, s_down, s_qkv, s_out, s_patch, s_red, s_conv, s_exp), vectors = finish(shares, sizes, [grad_feats, grad_text, *sums, *more])
     (s_bn1_gain, s_bn1_bias, s_bn2_gain, s_bn2_bias, s_bn3_gain, s_bn3_bias, s_b_patch, s_ln1_gain, s_ln1_bias, s_b_qv, s_b_out, s_ln2_gain, s_ln2_bias, s_b_up, s_b_down) = vectors
     return (
         output, grad_feats, grad_text,

time: 397 us -> 391 us (0.985)
  local copies, waits for them, and re-layouts: 8.34 us -> 0 us
    unnamed x23 -> x0, local copies, waits for them, and re-layouts: 8.34 us -> none
where the time goes in v3:
time: 391 us; the launch traced here: 385 us
  Pallas kernels  383 us (98%)
    pallas_call x1, Pallas kernels, stem_forward(): pl.pallas_call(functools.partial(stem_kernel, A, B, items, len(shards), s...  103 us
    pallas_call x1, Pallas kernels, attend_back(): pl.pallas_call(functools.partial(attend_back_kernel, A, B, n, patches, sl...  94.6 us
    pallas_call x1, Pallas kernels, stem_backward(): pl.pallas_call(functools.partial(stem_back_kernel, A, B, cuts, near_rows,...  78.2 us
    pallas_call x1, Pallas kernels, ffn(): pl.pallas_call(functools.partial(ffn_kernel, n, patches), grid=(hidden //...  67.1 us
    pallas_call x1, Pallas kernels, attend(): pl.pallas_call(functools.partial(attend_kernel, n, patches), grid=(steps,...  35.6 us

profile of v3, /device:TPU:0, one launch (start us, length us, event | category | flops | bytes accessed | tf_op | source)
XLA Modules:
  0.0 384.5 jit_solution(394165933839048639)
XLA Ops:
  0.7 102.6 %stem.1 = (bf16[2,2,4,2,32,768]{5,4,3,2,1,0:T(8,128)(2,1)}, bf16[2,2,4,2,24,2304]{5,4,3,2,1,0:T(8,128)(2,1)}, bf16[2,2,4,2,24,768]{5,4,3,2,1,0:T(8,128)(2,1)}, b...) custom-call(bf16[6,196,1024]{2,1,0:T(8,128)(2,1)} %refs_1_.1, ...), custom_call_target="tpu_custom_call" | custom-call | tf_op jit(solution)/shard_map/stem/pallas_call | solution.py:939
  103.3 35.6 %attend.1 = (f32[1632,768]{1,0:T(8,128)}, bf16[1632,768]{1,0:T(8,128)(2,1)}, bf16[1632,2304]{1,0:T(8,128)(2,1)}, bf16[1632,768]{1,0:T(8,128)(2,1)}, f32[1632,768]{1,0:T(8,128)}, /*index=5*/bf16[1632,768]{1,0:T(8,128)(2,1)}) custom-call(s32[6]{0:T(128)} %refs_0_.3, bf16[6,208,1024]{2,1,0:T(8,128)(2,1)} %get-tuple-element.94.act.refs_6_, ...), custom_call_target="tpu_custom_call" | custom-call | tf_op jit(solution)/shard_map/attend/pallas_call | solution.py:429
  139.0 67.1 %ffn.1 = (bf16[6,260,768]{2,1,0:T(8,128)(2,1)}, f32[1632,768]{1,0:T(8,128)}, bf16[768,3072]{1,0:T(8,128)(2,1)}, bf16[3072,768]{1,0:T(8,128)(2,1)}, f32[1,3072]{1,0:T(1,128)}, /*index=5*/f32[8,768]{1,0:T(8,128)}) custom-call(s32[6]{0:T(128)} %refs_0_.3, bf16[1632,768]{1,0:T(8,128)(2,1)} %get-tuple-element.99.h2, f32[1632,768]{1,0:T(8,128)} %get-tuple-element.100.x2_h, ...), custom_call_target="tpu_custom_call" | custom-call | tf_op jit(solution)/shard_map/ffn/pallas_call | solution.py:522
  206.1 94.6 %attend_back.1 = (f32[6,208,1024]{2,1,0:T(8,128)}, bf16[6,64,768]{2,1,0:T(8,128)(2,1)}, bf16[768,2304]{1,0:T(8,128)(2,1)}, bf16[768,768]{1,0:T(8,128)(2,1)}, bf1...) custom-call(s32[6]{0:T(128)} %refs_0_.3, ...), custom_call_target="tpu_custom_call" | custom-call | tf_op jit(solution)/shard_map/attend_back/pallas_call | solution.py:638
  300.7 78.2 %stem_back.1 = (bf16[6,196,1024]{2,1,0:T(8,128)(2,1)}, f32[16,128]{1,0:T(8,128)}, f32[24,2304]{1,0:T(8,128)}, f32[24,768]{1,0:T(8,128)}, f32[32,768]{1,0:T(8,128...) custom-call(f32[6,208,1024]{2,1,0:T(8,128)} %get-tuple-element.111.refs_0_, ...), custom_call_target="tpu_custom_call" | custom-call | tf_op jit(solution)/shard_map/stem_back/pallas_call | solution.py:1197
  378.9 5.2 %finish.1 = (bf16[6,196,1024]{2,1,0:T(8,128)(2,1)}, bf16[6,64,768]{2,1,0:T(8,128)(2,1)}, f32[24,3072]{1,0:T(8,128)}, f32[96,768]{1,0:T(8,128)}, f32[24,2304]{1,0...) custom-call(f32[16,128]{1,0:T(8,128)} %get-tuple-element.126.refs_0_, ...), custom_call_target="tpu_custom_call" | custom-call | tf_op jit(solution)/shard_map/finish/pallas_call | solution.py:1240

commit v4 on v3

--- a/solution.py
+++ b/solution.py
@@ -464,7 +464,7 @@
             dh[at] = jnp.zeros((rows, width), f32)
             return 0
 
-        lax.fori_loop(0, examples, body, 0)
+        lax.fori_loop(0, examples, body, 0, unroll=2)
         h2t[...] = h2[...].T
 
     def block(r, sums):
@@ -502,7 +502,7 @@
             return sums[0] + colsum(g), sums[1] + colsum(dy * hat), sums[2] + colsum(dy)
 
         zero = jnp.zeros((1, width), f32)
-        a, b, d = lax.fori_loop(0, examples, body, (zero, zero, zero))
+        a, b, d = lax.fori_loop(0, examples, body, (zero, zero, zero), unroll=2)
         small[0:1], small[1:2], small[2:3] = a, b, d
         small[3:8] = jnp.zeros((5, width), f32)
 
@@ -1112,7 +1112,7 @@
             gred[...] += dot_tn(feats[i], dr)
             return 0
 
-        lax.fori_loop(0, examples, body, 0)
+        lax.fori_loop(0, examples, body, 0, unroll=3)
         leave(m_red, gred, k_red, near_rows[0])
 
     def ninth(lo, hi):
@@ -1121,7 +1121,7 @@
             leave_feats(i).start()
             return 0
 
-        lax.fori_loop(lo, hi, body, 0)
+        lax.fori_loop(lo, hi, body, 0, unroll=True)
 
     def finish():
         v = vec_sum.end()
@@ -1265,7 +1265,7 @@
     full_patch, full_qkv, full_out, full_up, full_down = far
     act, red, conv, expand, params, stats, full_red, full_conv, full_exp = near
     x, h1, qkv, o, x2, h2 = attend(lengths, act, text, full_patch, full_qkv, full_out, params, patches, 2)
-    output, dx2, g_up, g_down, small_b, small_f = ffn(lengths, h2, x2, cotangent, full_up, full_down, params, patches, 2, 512)
+    output, dx2, g_up, g_down, small_b, small_f = ffn(lengths, h2, x2, cotangent, full_up, full_down, params, patches, 2, 1024)
     inside = w_qkv.shape[0] >= 16
     first = [g_up, g_down] if inside else []
     dact, grad_text, g_qkv, g_out, g_patch, small_a, small_q, *sums = attend_back(

time: 391 us -> 390 us (level)
  no operation moved by 1% of the time
where the time goes in v4:
time: 390 us; the launch traced here: 383 us
  Pallas kernels  382 us (98%)
    pallas_call x1, Pallas kernels, stem_forward(): pl.pallas_call(functools.partial(stem_kernel, A, B, items, len(shards), s...  103 us
    pallas_call x1, Pallas kernels, attend_back(): pl.pallas_call(functools.partial(attend_back_kernel, A, B, n, patches, sl...  94.3 us
    pallas_call x1, Pallas kernels, stem_backward(): pl.pallas_call(functools.partial(stem_back_kernel, A, B, cuts, near_rows,...  78.1 us
    pallas_call x1, Pallas kernels, ffn(): pl.pallas_call(functools.partial(ffn_kernel, n, patches), grid=(hidden //...  66.4 us
    pallas_call x1, Pallas kernels, attend(): pl.pallas_call(functools.partial(attend_kernel, n, patches), grid=(steps,...  35.3 us

profile of v4, /device:TPU:0, one launch (start us, length us, event | category | flops | bytes accessed | tf_op | source)
XLA Modules:
  0.0 383.0 jit_solution(15165558961822063448)
XLA Ops:
  0.7 102.7 %stem.1 = (bf16[2,2,4,2,32,768]{5,4,3,2,1,0:T(8,128)(2,1)}, bf16[2,2,4,2,24,2304]{5,4,3,2,1,0:T(8,128)(2,1)}, bf16[2,2,4,2,24,768]{5,4,3,2,1,0:T(8,128)(2,1)}, b...) custom-call(bf16[6,196,1024]{2,1,0:T(8,128)(2,1)} %refs_1_.1, ...), custom_call_target="tpu_custom_call" | custom-call | tf_op jit(solution)/shard_map/stem/pallas_call | solution.py:939
  103.3 35.3 %attend.1 = (f32[1632,768]{1,0:T(8,128)}, bf16[1632,768]{1,0:T(8,128)(2,1)}, bf16[1632,2304]{1,0:T(8,128)(2,1)}, bf16[1632,768]{1,0:T(8,128)(2,1)}, f32[1632,768]{1,0:T(8,128)}, /*index=5*/bf16[1632,768]{1,0:T(8,128)(2,1)}) custom-call(s32[6]{0:T(128)} %refs_0_.3, bf16[6,208,1024]{2,1,0:T(8,128)(2,1)} %get-tuple-element.94.act.refs_6_, ...), custom_call_target="tpu_custom_call" | custom-call | tf_op jit(solution)/shard_map/attend/pallas_call | solution.py:429
  138.7 66.4 %ffn.1 = (bf16[6,260,768]{2,1,0:T(8,128)(2,1)}, f32[1632,768]{1,0:T(8,128)}, bf16[768,3072]{1,0:T(8,128)(2,1)}, bf16[3072,768]{1,0:T(8,128)(2,1)}, f32[1,3072]{1,0:T(1,128)}, /*index=5*/f32[8,768]{1,0:T(8,128)}) custom-call(s32[6]{0:T(128)} %refs_0_.3, bf16[1632,768]{1,0:T(8,128)(2,1)} %get-tuple-element.99.h2, f32[1632,768]{1,0:T(8,128)} %get-tuple-element.100.x2_h, ...), custom_call_target="tpu_custom_call" | custom-call | tf_op jit(solution)/shard_map/ffn/pallas_call | solution.py:522
  205.1 94.3 %attend_back.1 = (f32[6,208,1024]{2,1,0:T(8,128)}, bf16[6,64,768]{2,1,0:T(8,128)(2,1)}, bf16[768,2304]{1,0:T(8,128)(2,1)}, bf16[768,768]{1,0:T(8,128)(2,1)}, bf1...) custom-call(s32[6]{0:T(128)} %refs_0_.3, ...), custom_call_target="tpu_custom_call" | custom-call | tf_op jit(solution)/shard_map/attend_back/pallas_call | solution.py:638
  299.4 78.1 %stem_back.1 = (bf16[6,196,1024]{2,1,0:T(8,128)(2,1)}, f32[16,128]{1,0:T(8,128)}, f32[24,2304]{1,0:T(8,128)}, f32[24,768]{1,0:T(8,128)}, f32[32,768]{1,0:T(8,128...) custom-call(f32[6,208,1024]{2,1,0:T(8,128)} %get-tuple-element.111.refs_0_, ...), custom_call_target="tpu_custom_call" | custom-call | tf_op jit(solution)/shard_map/stem_back/pallas_call | solution.py:1197
  377.5 5.2 %finish.1 = (bf16[6,196,1024]{2,1,0:T(8,128)(2,1)}, bf16[6,64,768]{2,1,0:T(8,128)(2,1)}, f32[24,3072]{1,0:T(8,128)}, f32[96,768]{1,0:T(8,128)}, f32[24,2304]{1,0...) custom-call(f32[16,128]{1,0:T(8,128)} %get-tuple-element.126.refs_0_, ...), custom_call_target="tpu_custom_call" | custom-call | tf_op jit(solution)/shard_map/finish/pallas_call | solution.py:1240
